TPU v7x, 32 devices: a whole 2x2x4 slice. The times are simulated.
32 devices in a mesh: dp: 8 (over z, x), tensor: 4 (over y, core).
Axes of the slice: x: 2, y: 2, z: 4, core: 2. Of those that a mesh axis runs over, the one named last changes fastest.
Arguments:
- tokens: bfloat16 [8192, 2048], P('dp'), may hold values from -6 to 6
- out_grad: bfloat16 [8192, 2048], P('dp'), may hold values from -6 to 6
- starts: int32 [5], replicated, may hold values from 0 to 7936, as said below
- attn_gain: bfloat16 [2048], P('dp'), may hold values from 0.5 to 1.5
- w_query: bfloat16 [2048, 1024], P('dp', 'tensor'), may hold values from -0.125 to 0.125
- w_key: bfloat16 [2048, 1024], P('dp', 'tensor'), may hold values from -0.125 to 0.125
- w_value: bfloat16 [2048, 2048], P('dp', 'tensor'), may hold values from -0.125 to 0.125
- w_outgate: bfloat16 [2048, 2048], P('dp', 'tensor'), may hold values from -0.125 to 0.125
- w_decay_down: bfloat16 [2048, 16], P('dp'), may hold values from -0.125 to 0.125
- w_decay_up: bfloat16 [16, 1024], P(None, ('tensor', 'dp')), may hold values from -1.5 to 1.5
- decay_bias: bfloat16 [1024], P(('tensor', 'dp')), may hold values from -1 to 10
- head_gain: bfloat16 [2048], P(('tensor', 'dp')), may hold values from 0.5 to 1.5
- w_output: bfloat16 [2048, 2048], P('tensor', 'dp'), may hold values from -0.25 to 0.25
- ffn_gain: bfloat16 [2048], P('dp'), may hold values from 0.5 to 1.5
- w_gate: bfloat16 [2048, 5632], P('dp', 'tensor'), may hold values from -0.125 to 0.125
- w_up: bfloat16 [2048, 5632], P('dp', 'tensor'), may hold values from -0.125 to 0.125
- w_down: bfloat16 [5632, 2048], P('tensor', 'dp'), may hold values from -0.21875 to 0.21875
Outputs:
- output: bfloat16 [8192, 2048], P('dp')
- input_grad: float32 [8192, 2048], P('dp')
- grad_attn_gain: float32 [2048], P('dp')
- grad_w_query: float32 [2048, 1024], P('dp', 'tensor')
- grad_w_key: float32 [2048, 1024], P('dp', 'tensor')
- grad_w_value: float32 [2048, 2048], P('dp', 'tensor')
- grad_w_outgate: float32 [2048, 2048], P('dp', 'tensor')
- grad_w_decay_down: float32 [2048, 16], P('dp')
- grad_w_decay_up: float32 [16, 1024], P(None, ('tensor', 'dp'))
- grad_decay_bias: float32 [1024], P(('tensor', 'dp'))
- grad_head_gain: float32 [2048], P(('tensor', 'dp'))
- grad_w_output: float32 [2048, 2048], P('tensor', 'dp')
- grad_ffn_gain: float32 [2048], P('dp')
- grad_w_gate: float32 [2048, 5632], P('dp', 'tensor')
- grad_w_up: float32 [2048, 5632], P('dp', 'tensor')
- grad_w_down: float32 [5632, 2048], P('tensor', 'dp')
Inputs may be any that keep to these rules, and one draw needn't show every extreme that they name: `starts`: strictly increasing, the first is 0; the last is 7936.
All inputs are finite; a program needn't handle non-finite values.
Results may differ from a plain program's by a relative error of at most 0.018.
Values may be sent and summed in bfloat16 or wider, within the bound.
No kernel may reach another device: no remote copies, remote signals or barrier semaphores. Data moves between devices by JAX's collectives and lax.ppermute only.
A program may use at most 256 MiB of HBM per device.

v0:
```python
import jax
import jax.numpy as jnp
from jax import lax
from jax.sharding import PartitionSpec as P

DK = 256
DV = 512
GROUP = 64


HIGHEST_PRECISION = lax.Precision.HIGHEST
EPSILON = 1e-06
GATE_NORMALIZER = 16.0


def carried_in(value, axis, join, neutral, backward):
    count, mine = (lax.axis_size(axis), lax.axis_index(axis))
    pieces = jax.tree.map(lambda part: lax.all_gather(part, axis), value)
    if backward:
        pieces = jax.tree.map(lambda part: part[::-1], pieces)
        mine = count - 1 - mine
    total = jax.tree.map(
        lambda part, zero: jnp.full_like(part, 0) + jnp.asarray(zero, part.dtype), value, neutral
    )

    def turn(position, total):
        longer = join(total, jax.tree.map(lambda part: part[position], pieces))
        return jax.tree.map(lambda new, old: jnp.where(position < mine, new, old), longer, total)

    return lax.fori_loop(0, count - 1, turn, total)


def rms_parts(values):
    inverse = lax.rsqrt(jnp.mean(values * values, axis=-1, keepdims=True) + EPSILON)
    return (values * inverse, inverse)


def norm_back(d_normed, gains, unit, inverse):
    scaled = d_normed * gains
    return inverse * (scaled - unit * jnp.mean(scaled * unit, axis=-1, keepdims=True))


def group_step(carried, inputs):
    block_q, block_k, block_v, block_decay, block_segment, segment_prev = inputs
    cumulative = jnp.cumsum(block_decay, axis=0)
    q_scaled = block_q * jnp.exp(cumulative)
    k_scaled = block_k * jnp.exp(-cumulative)
    scores = jnp.einsum("thc,shc->hts", q_scaled, k_scaled, precision=HIGHEST_PRECISION)
    length = block_q.shape[0]
    places = jnp.arange(length)
    allowed = (places[None, :] <= places[:, None]) & (
        block_segment[None, :] == block_segment[:, None]
    )
    scores = jnp.where(allowed[None], scores, 0.0)
    within = jnp.einsum("hts,shv->thv", scores, block_v, precision=HIGHEST_PRECISION)
    carry_on = (block_segment == segment_prev).astype(jnp.float32)
    outside = (
        jnp.einsum("thc,hcv->thv", q_scaled, carried, precision=HIGHEST_PRECISION)
        * carry_on[:, None, None]
    )
    at_end = cumulative[-1]
    same_last = (block_segment == block_segment[-1]).astype(jnp.float32)
    k_end = block_k * jnp.exp(at_end[None] - cumulative) * same_last[:, None, None]
    updated = carried * (jnp.exp(at_end) * carry_on[-1])[:, :, None]
    updated = updated + jnp.einsum("shc,shv->hcv", k_end, block_v, precision=HIGHEST_PRECISION)
    return (updated, within + outside)


def own_part(part_q, part_k, part_v, part_decay, segment, segment_before):
    count = part_q.shape[0]
    heads_here = part_q.shape[1]
    blocks = count // GROUP
    previous = jnp.concatenate([segment_before[None], segment[:-1]])[::GROUP]
    initial = jnp.zeros((heads_here, DK, DV), jnp.float32)
    inputs = (
        part_q.reshape(blocks, GROUP, heads_here, DK),
        part_k.reshape(blocks, GROUP, heads_here, DK),
        part_v.reshape(blocks, GROUP, heads_here, DV),
        part_decay.reshape(blocks, GROUP, heads_here, DK),
        segment.reshape(blocks, GROUP),
        previous,
    )
    finished, outputs = lax.scan(jax.checkpoint(group_step), initial, inputs)
    alive = (segment == segment_before).astype(jnp.float32)
    reach = jnp.exp(jnp.cumsum(part_decay, axis=0)) * alive[:, None, None]
    return (outputs.reshape(count, heads_here, DV), finished, reach)


def combine_maps(earlier, later):
    return (earlier[0] * later[0], later[0][..., None] * earlier[1] + later[1])


def chain_states(decay_part, state_part, backward):
    identity = (jnp.ones_like(decay_part), jnp.zeros_like(state_part))
    return carried_in((decay_part, state_part), "dp", combine_maps, identity, backward)[1]


def shards(
    tokens,
    out_grad,
    starts,
    attn_gain,
    w_query,
    w_key,
    w_value,
    w_outgate,
    w_decay_down,
    w_decay_up,
    decay_bias,
    head_gain,
    w_output,
    ffn_gain,
    w_gate,
    w_up,
    w_down,
):
    (
        full_query,
        full_key,
        full_value,
        full_outgate,
        full_down_rank,
        full_up_rank,
        full_bias,
        full_head_gain,
        full_output,
        full_attn_gain,
    ) = (
        lax.all_gather(w_query, "dp", axis=0, tiled=True),
        lax.all_gather(w_key, "dp", axis=0, tiled=True),
        lax.all_gather(w_value, "dp", axis=0, tiled=True),
        lax.all_gather(w_outgate, "dp", axis=0, tiled=True),
        lax.all_gather(w_decay_down, "dp", axis=0, tiled=True),
        lax.all_gather(w_decay_up, "dp", axis=1, tiled=True),
        lax.all_gather(decay_bias, "dp", axis=0, tiled=True),
        lax.all_gather(head_gain, "dp", axis=0, tiled=True),
        lax.all_gather(w_output, "dp", axis=1, tiled=True),
        lax.all_gather(attn_gain, "dp", axis=0, tiled=True),
    )
    full_gate, full_up, full_down, full_ffn_gain = (
        lax.all_gather(w_gate, "dp", axis=0, tiled=True),
        lax.all_gather(w_up, "dp", axis=0, tiled=True),
        lax.all_gather(w_down, "dp", axis=1, tiled=True),
        lax.all_gather(ffn_gain, "dp", axis=0, tiled=True),
    )
    count = tokens.shape[0]
    share = count // lax.axis_size("tensor")
    share_start = lax.axis_index("tensor") * share
    heads_here = full_query.shape[1] // DK
    scaling = DK ** (-0.5)
    gain_one = full_attn_gain.astype(jnp.float32)
    gain_two = full_ffn_gain.astype(jnp.float32)
    head_gains = full_head_gain.astype(jnp.float32).reshape(heads_here, DV)
    up_rank = full_up_rank.astype(jnp.float32)
    inputs = tokens.astype(jnp.float32)
    unit_one, inverse_one = rms_parts(inputs)
    normed = (unit_one * gain_one).astype(jnp.bfloat16)
    queries = jnp.dot(normed, full_query, preferred_element_type=jnp.float32)
    keys_flat = jnp.dot(normed, full_key, preferred_element_type=jnp.float32)
    values_flat = jnp.dot(normed, full_value, preferred_element_type=jnp.float32)
    outgate = jnp.dot(normed, full_outgate, preferred_element_type=jnp.float32)
    decay_low = jnp.dot(normed, full_down_rank, preferred_element_type=jnp.float32)
    decay_logit = jnp.dot(decay_low, up_rank, precision=HIGHEST_PRECISION) + full_bias.astype(
        jnp.float32
    )
    log_decay = jax.nn.log_sigmoid(decay_logit) / GATE_NORMALIZER
    scaled_q = (queries * scaling).reshape(count, heads_here, DK)
    keys_in = keys_flat.reshape(count, heads_here, DK)
    values_in = values_flat.reshape(count, heads_here, DV)
    decay_heads = log_decay.reshape(count, heads_here, DK)
    first_place = lax.axis_index("dp") * count
    positions = first_place + jnp.arange(count, dtype=jnp.int32)
    segment = jnp.sum((starts[None, :] <= positions[:, None]).astype(jnp.int32), axis=1) - 1
    segment_before = jnp.sum((starts <= first_place - 1).astype(jnp.int32)) - 1
    within, at_end, reach = own_part(
        scaled_q, keys_in, values_in, decay_heads, segment, segment_before
    )
    q_reach = scaled_q * reach
    device_decay = reach[-1]
    incoming = chain_states(device_decay, at_end, False)
    mixed = within + jnp.einsum("thc,hcv->thv", q_reach, incoming, precision=HIGHEST_PRECISION)
    head_unit, head_inverse = rms_parts(mixed)
    head_out = head_unit * head_gains
    outgate_heads = outgate.reshape(count, heads_here, DV)
    outgate_sigmoid = jax.nn.sigmoid(outgate_heads)
    outgate_act = outgate_heads * outgate_sigmoid
    gated = (head_out * outgate_act).reshape(count, heads_here * DV).astype(jnp.bfloat16)
    branch_part = jnp.dot(gated, full_output, preferred_element_type=jnp.float32)
    out_grad_float = out_grad.astype(jnp.float32)
    branch = lax.psum(branch_part, "tensor")
    hidden_in = inputs + branch
    unit_two, inverse_two = rms_parts(hidden_in)
    normed_two = (unit_two * gain_two).astype(jnp.bfloat16)
    gate_pre = jnp.dot(normed_two, full_gate, preferred_element_type=jnp.float32)
    up_proj = jnp.dot(normed_two, full_up, preferred_element_type=jnp.float32)
    gate_sigmoid = jax.nn.sigmoid(gate_pre)
    gate_silu = gate_pre * gate_sigmoid
    hidden = (gate_silu * up_proj).astype(jnp.bfloat16)
    ffn_part = jnp.dot(hidden, full_down, preferred_element_type=jnp.float32)
    ffn_out = lax.psum(ffn_part.astype(jnp.bfloat16), "tensor").astype(jnp.float32)
    output = (hidden_in + ffn_out).astype(jnp.bfloat16)
    grad_down = jnp.einsum("tf,td->fd", hidden, out_grad, preferred_element_type=jnp.float32)
    d_hidden = jnp.einsum("td,fd->tf", out_grad, full_down, preferred_element_type=jnp.float32)
    d_gate = (d_hidden * up_proj * gate_sigmoid * (1.0 + gate_pre * (1.0 - gate_sigmoid))).astype(
        jnp.bfloat16
    )
    d_up = (d_hidden * gate_silu).astype(jnp.bfloat16)
    grad_gate = jnp.einsum("td,tf->df", normed_two, d_gate, preferred_element_type=jnp.float32)
    grad_up = jnp.einsum("td,tf->df", normed_two, d_up, preferred_element_type=jnp.float32)
    d_normed_part = jnp.einsum("tf,df->td", d_gate, full_gate, preferred_element_type=jnp.float32)
    d_normed_part = d_normed_part + jnp.einsum(
        "tf,df->td", d_up, full_up, preferred_element_type=jnp.float32
    )
    d_normed_two = lax.psum(d_normed_part, "tensor")
    ffn_gain_part = jnp.sum(
        lax.dynamic_slice_in_dim(d_normed_two * unit_two, share_start, share, 0), axis=0
    )
    d_hidden_in = out_grad_float + norm_back(d_normed_two, gain_two, unit_two, inverse_two)
    d_branch = d_hidden_in.astype(jnp.bfloat16)
    grad_output = jnp.einsum("tv,td->vd", gated, d_branch, preferred_element_type=jnp.float32)
    d_gated = jnp.einsum("td,vd->tv", d_branch, full_output, preferred_element_type=jnp.float32)
    d_gated = d_gated.reshape(count, heads_here, DV)
    d_head_out = d_gated * outgate_act
    d_outgate = (
        d_gated * head_out * outgate_sigmoid * (1.0 + outgate_heads * (1.0 - outgate_sigmoid))
    )
    grad_head_gain = jnp.sum(d_head_out * head_unit, axis=0).reshape(heads_here * DV)
    d_mixed = norm_back(d_head_out, head_gains, head_unit, head_inverse)
    own_grad = jnp.einsum("thc,thv->hcv", q_reach, d_mixed, precision=HIGHEST_PRECISION)
    grad_later = chain_states(device_decay, own_grad, True)

    def mixer(part_q, part_k, part_v, part_decay, part_in):
        inner, finish, reach_inner = own_part(
            part_q, part_k, part_v, part_decay, segment, segment_before
        )
        combined = inner + jnp.einsum(
            "thc,hcv->thv", part_q * reach_inner, part_in, precision=HIGHEST_PRECISION
        )
        return (combined, reach_inner[-1][:, :, None] * part_in + finish)

    unused_value, pullback = jax.vjp(mixer, scaled_q, keys_in, values_in, decay_heads, incoming)
    d_scaled_q, d_keys, d_values, d_decay, unused_grad = pullback((d_mixed, grad_later))
    d_query_low = (d_scaled_q * scaling).reshape(count, heads_here * DK).astype(jnp.bfloat16)
    d_key_low = d_keys.reshape(count, heads_here * DK).astype(jnp.bfloat16)
    d_value_low = d_values.reshape(count, heads_here * DV).astype(jnp.bfloat16)
    d_outgate_low = d_outgate.reshape(count, heads_here * DV).astype(jnp.bfloat16)
    d_logit = (
        d_decay.reshape(count, heads_here * DK) * jax.nn.sigmoid(-decay_logit) / GATE_NORMALIZER
    )
    grad_up_rank = jnp.einsum("tr,tk->rk", decay_low, d_logit, precision=HIGHEST_PRECISION)
    grad_bias = jnp.sum(d_logit, axis=0)
    d_rank_part = jnp.einsum("tk,rk->tr", d_logit, up_rank, precision=HIGHEST_PRECISION)
    d_first_part = jnp.einsum(
        "tk,dk->td", d_query_low, full_query, preferred_element_type=jnp.float32
    )
    d_first_part = d_first_part + jnp.einsum(
        "tk,dk->td", d_key_low, full_key, preferred_element_type=jnp.float32
    )
    d_first_part = d_first_part + jnp.einsum(
        "tv,dv->td", d_value_low, full_value, preferred_element_type=jnp.float32
    )
    d_first_part = d_first_part + jnp.einsum(
        "tv,dv->td", d_outgate_low, full_outgate, preferred_element_type=jnp.float32
    )
    grad_query = jnp.einsum("td,tk->dk", normed, d_query_low, preferred_element_type=jnp.float32)
    grad_key = jnp.einsum("td,tk->dk", normed, d_key_low, preferred_element_type=jnp.float32)
    grad_value = jnp.einsum("td,tv->dv", normed, d_value_low, preferred_element_type=jnp.float32)
    grad_outgate = jnp.einsum(
        "td,tv->dv", normed, d_outgate_low, preferred_element_type=jnp.float32
    )
    d_normed_sum, d_rank_sum, grad_ffn_gain = (
        lax.psum(d_first_part.astype(jnp.bfloat16), "tensor").astype(jnp.float32),
        lax.psum(d_rank_part.astype(jnp.bfloat16), "tensor").astype(jnp.float32),
        lax.psum(ffn_gain_part.astype(jnp.bfloat16), "tensor").astype(jnp.float32),
    )
    d_rank_low = d_rank_sum.astype(jnp.bfloat16)
    d_normed = d_normed_sum + jnp.einsum(
        "tr,dr->td", d_rank_low, full_down_rank, preferred_element_type=jnp.float32
    )
    grad_down_rank = jnp.einsum("td,tr->dr", normed, d_rank_low, preferred_element_type=jnp.float32)
    grad_attn_gain = jnp.sum(d_normed * unit_one, axis=0)
    input_grad = d_hidden_in + norm_back(d_normed, gain_one, unit_one, inverse_one)
    (
        sum_query,
        sum_key,
        sum_value,
        sum_outgate,
        sum_down_rank,
        sum_up_rank,
        sum_bias,
        sum_head_gain,
        sum_output,
        sum_attn_gain,
        sum_gate,
        sum_up,
        sum_down,
        sum_ffn_gain,
    ) = (
        lax.psum_scatter(
            grad_query.astype(jnp.bfloat16), "dp", scatter_dimension=0, tiled=True
        ).astype(jnp.float32),
        lax.psum_scatter(
            grad_key.astype(jnp.bfloat16), "dp", scatter_dimension=0, tiled=True
        ).astype(jnp.float32),
        lax.psum_scatter(
            grad_value.astype(jnp.bfloat16), "dp", scatter_dimension=0, tiled=True
        ).astype(jnp.float32),
        lax.psum_scatter(
            grad_outgate.astype(jnp.bfloat16), "dp", scatter_dimension=0, tiled=True
        ).astype(jnp.float32),
        lax.psum_scatter(
            grad_down_rank.astype(jnp.bfloat16), "dp", scatter_dimension=0, tiled=True
        ).astype(jnp.float32),
        lax.psum_scatter(
            grad_up_rank.astype(jnp.bfloat16), "dp", scatter_dimension=1, tiled=True
        ).astype(jnp.float32),
        lax.psum_scatter(
            grad_bias.astype(jnp.bfloat16), "dp", scatter_dimension=0, tiled=True
        ).astype(jnp.float32),
        lax.psum_scatter(
            grad_head_gain.astype(jnp.bfloat16), "dp", scatter_dimension=0, tiled=True
        ).astype(jnp.float32),
        lax.psum_scatter(
            grad_output.astype(jnp.bfloat16), "dp", scatter_dimension=1, tiled=True
        ).astype(jnp.float32),
        lax.psum_scatter(
            grad_attn_gain.astype(jnp.bfloat16), "dp", scatter_dimension=0, tiled=True
        ).astype(jnp.float32),
        lax.psum_scatter(
            grad_gate.astype(jnp.bfloat16), "dp", scatter_dimension=0, tiled=True
        ).astype(jnp.float32),
        lax.psum_scatter(
            grad_up.astype(jnp.bfloat16), "dp", scatter_dimension=0, tiled=True
        ).astype(jnp.float32),
        lax.psum_scatter(
            grad_down.astype(jnp.bfloat16), "dp", scatter_dimension=1, tiled=True
        ).astype(jnp.float32),
        lax.psum_scatter(
            grad_ffn_gain.astype(jnp.bfloat16), "dp", scatter_dimension=0, tiled=True
        ).astype(jnp.float32),
    )
    return (
        output,
        input_grad,
        sum_attn_gain,
        sum_query,
        sum_key,
        sum_value,
        sum_outgate,
        sum_down_rank,
        sum_up_rank,
        sum_bias,
        sum_head_gain,
        sum_output,
        sum_ffn_gain,
        sum_gate,
        sum_up,
        sum_down,
    )


def solution(mesh):
    return jax.shard_map(
        shards,
        mesh=mesh,
        in_specs=(
            P("dp", None),
            P("dp", None),
            P(),
            P("dp"),
            P("dp", "tensor"),
            P("dp", "tensor"),
            P("dp", "tensor"),
            P("dp", "tensor"),
            P("dp", None),
            P(None, ("tensor", "dp")),
            P(("tensor", "dp")),
            P(("tensor", "dp")),
            P("tensor", "dp"),
            P("dp"),
            P("dp", "tensor"),
            P("dp", "tensor"),
            P("tensor", "dp"),
        ),
        out_specs=(
            P("dp", None),
            P("dp", None),
            P("dp"),
            P("dp", "tensor"),
            P("dp", "tensor"),
            P("dp", "tensor"),
            P("dp", "tensor"),
            P("dp", None),
            P(None, ("tensor", "dp")),
            P(("tensor", "dp")),
            P(("tensor", "dp")),
            P("tensor", "dp"),
            P("dp"),
            P("dp", "tensor"),
            P("dp", "tensor"),
            P("tensor", "dp"),
        ),
        check_vma=False,
    )
```

profile of v0, /device:TPU:0, one launch (start us, length us, event | category | flops | bytes accessed | tf_op | source)
XLA Modules:
  0.0 2135.6 jit_solution(12661148474316138582)
XLA Ops:
  10.8 22.3 %all-gather.2 = bf16[8,1,256]{2,1,0:T(2,128)(2,1)S(1)} all-gather(bf16[1,1,256]{2,1,0:T(2,128)(2,1)S(1)} %reshape.914), channel_id=1, replica_groups=mesh['dp'=8,'tensor'=4] {'dp'}, dimensions={0}, use_global_device_ids=true | all-gather | bytes 4608 | tf_op jit(solution)/shard_map/all_gather | solution.py:138
  36.2 30.6 %all_gather.59 = bf16[2048,16]{0,1:T(8,128)(2,1)S(1)} all-gather(bf16[256,16]{0,1:T(8,128)(2,1)S(1)} %copy-done.43), channel_id=1, replica_groups=mesh['dp'=8,'tensor'=4] {'dp'}, dimensions={0}, use_global_device_ids=true | all-gather | bytes 73728 | tf_op jit(solution)/shard_map/all_gather | solution.py:133
  69.2 17.4 all-reduce.9
  86.6 30.9 %all-gather.3 = bf16[8,32,16]{1,2,0:T(8,128)(2,1)S(1)} all-gather(bf16[1,32,16]{1,2,0:T(8,128)(2,1)S(1)} %bitcast.769), channel_id=1, replica_groups=mesh['dp'=8,'tensor'=4] {'dp'}, dimensions={0}, use_global_device_ids=true | all-gather | bytes 9216 | tf_op jit(solution)/shard_map/all_gather | solution.py:134
  152.2 144.5 %while.82 = (s32[]{:T(128)}, f32[1,256,512]{2,1,0:T(8,128)S(1)}, f32[16,64,1,512]{3,1,2,0:T(8,128)}, f32[16,64,1,256]{3,2,1,0:T(1,128)}, s32[16,64]{1,0:T(8,128)...) while((s32[]{:T(128)}, f32[1,256,512]{2,1,0:T(8,128)S(1)}, ...), condition=%wide.region_5.6_spmd.clone.clone, body=%wide.region_3.5_spmd.clone.sunk.clone | while | flops 240812544 | bytes 3516064 | solution.py:83
  302.1 18.1 all_gather.65
  320.2 6.5 fusion.154
  329.7 39.9 %all-gather.32.cloned.1.call-done = f32[8,256,512]{2,1,0:T(8,128)} async-done(((f32[1,256,512]{2,1,0:T(8,128)}), f32[8,256,512]{2,1,0:T(8,128)}) %all-gather.32.cloned.1.call-update) | async-done | bytes 4194320 | tf_op jit(solution)/shard_map/all_gather | solution.py:18
  369.6 8.5 while.83
  378.1 6.0 multiply_reduce_fusion.3
  385.8 35.1 %all-gather.24.cloned.1.call-done = bf16[512,2048]{1,0:T(8,128)(2,1)} async-done(((bf16[512,256]{1,0:T(8,128)(2,1)}), bf16[512,2048]{1,0:T(8,128)(2,1)}) %all-gather.24.cloned.1.call-update) | async-done | bytes 2097168 | tf_op jit(solution)/shard_map/all_gather | solution.py:137
  420.9 7.7 fusion.155
  430.8 17.7 all-gather.4
  448.5 131.3 %all-reduce.15.cloned.1.call-done = f32[1024,2048]{1,0:T(8,128)} async-done(((f32[1024,2048]{1,0:T(8,128)}), f32[1024,2048]{1,0:T(8,128)}) %all-reduce.15.cloned.1.call-update) | async-done | bytes 8388624 | tf_op jit(solution)/shard_map/psum | solution.py:190
  588.1 6.1 multiply_convert_fusion
  594.1 80.7 %all-gather.26.cloned.1.call-done = bf16[2048,1408]{1,0:T(8,128)(2,1)} async-done(((bf16[256,1408]{1,0:T(8,128)(2,1)}), bf16[2048,1408]{1,0:T(8,128)(2,1)}) %all-gather.26.cloned.1.call-update) | async-done | bytes 5767184 | tf_op jit(solution)/shard_map/all_gather | solution.py:141
  674.8 11.8 fusion.156
  686.6 81.3 %all-gather.28.cloned.1.call-done = bf16[2048,1408]{1,0:T(8,128)(2,1)} async-done(((bf16[256,1408]{1,0:T(8,128)(2,1)}), bf16[2048,1408]{1,0:T(8,128)(2,1)}) %all-gather.28.cloned.1.call-update) | async-done | bytes 5767184 | tf_op jit(solution)/shard_map/all_gather | solution.py:142
  767.9 11.7 fusion.157
  779.6 82.0 %all-gather.30.cloned.1.call-done = bf16[1408,2048]{1,0:T(8,128)(2,1)} async-done(((bf16[1408,256]{1,0:T(8,128)(2,1)}), bf16[1408,2048]{1,0:T(8,128)(2,1)}) %all-gather.30.cloned.1.call-update) | async-done | bytes 5767184 | tf_op jit(solution)/shard_map/all_gather | solution.py:143
  861.6 15.6 multiply_convert_fusion.1
  877.2 10.9 fusion.158
  888.1 9.1 convolution_add_fusion.2
  897.2 151.2 %all-reduce.17.cloned.1.call-done = f32[1024,2048]{1,0:T(8,128)} async-done(((f32[1024,2048]{1,0:T(8,128)}), f32[1024,2048]{1,0:T(8,128)}) %all-reduce.17.cloned.1.call-update) | async-done | bytes 8388624 | tf_op jit(solution)/shard_map/psum | solution.py:214
  1048.4 6.8 multiply_reduce_fusion.1
  1056.6 6.2 multiply_add_fusion.1
  1076.0 7.0 convolution_convert_fusion.4
  1083.1 6.2 convolution_convert_fusion.5
  1089.3 11.0 convolution_convert_fusion.2
  1101.6 11.1 convolution_convert_fusion.1
  1113.3 141.4 %while.85 = (s32[]{:T(128)}, f32[1,256,512]{2,1,0:T(8,128)S(1)}, f32[16,1,256,512]{3,2,1,0:T(8,128)}, f32[16,64,1,256]{3,2,1,0:T(1,128)}, s32[16,64]{1,0:T(8,128...) while((s32[]{:T(128)}, f32[1,256,512]{2,1,0:T(8,128)S(1)}, ...), condition=%wide.region_21.22_spmd.clone.clone, body=%wide.region_19.21_spmd.clone.sunk.clone | while | flops 102269376 | bytes 2892243 | solution.py:83
  1254.7 10.5 convolution_convert_fusion
  1268.3 6.0 fusion.110
  1279.1 8.5 while.84
  1289.9 264.3 %while.81 = (s32[]{:T(128)}, f32[1,256,512]{1,2,0:T(8,128)S(1)}, f32[16,64,1,256]{3,1,2,0:T(8,128)}, bf16[16,64,1,256]{3,1,2,0:T(8,128)(2,1)S(1)}, bf16[16,64,1,...) while((s32[]{:T(128)}, f32[1,256,512]{1,2,0:T(8,128)S(1)}, ...), condition=%wide.region_27.28_spmd.clone, body=%wide.region_22.27_spmd.sunk.clone | while | flops 493994752 | bytes 10998497 | solution.py:83
  1565.5 11.1 psum.46
  1584.8 11.2 convolution_convert_fusion.3
  1612.2 9.3 add_convert_fusion
  1643.7 50.4 %reduce-scatter.31.cloned.1.call-done = bf16[32,16]{1,0:T(8,128)(2,1)} async-done(((bf16[256,16]{1,0:T(8,128)(2,1)}), bf16[32,16]{1,0:T(8,128)(2,1)}) %reduce-scatter.31.cloned.1.call-update) | async-done | bytes 1040
  1695.5 55.0 %reduce-scatter.21.cloned.1.call-done = bf16[256,16]{0,1:T(8,128)(2,1)} async-done(((bf16[2048,16]{0,1:T(8,128)(2,1)}), bf16[256,16]{0,1:T(8,128)(2,1)}) %reduce-scatter.21.cloned.1.call-update) | async-done | bytes 8208 | tf_op jit(solution)/shard_map/reduce_scatter | solution.py:311
  1751.8 64.5 %reduce-scatter.13.cloned.1.call-done = bf16[256,256]{1,0:T(8,128)(2,1)} async-done(((bf16[2048,256]{1,0:T(8,128)(2,1)}), bf16[256,256]{1,0:T(8,128)(2,1)}) %reduce-scatter.13.cloned.1.call-update) | async-done | bytes 131088 | tf_op jit(solution)/shard_map/reduce_scatter | solution.py:299
  1818.0 64.5 %reduce-scatter.15.cloned.1.call-done = bf16[256,256]{1,0:T(8,128)(2,1)} async-done(((bf16[2048,256]{1,0:T(8,128)(2,1)}), bf16[256,256]{1,0:T(8,128)(2,1)}) %reduce-scatter.15.cloned.1.call-update) | async-done | bytes 131088 | tf_op jit(solution)/shard_map/reduce_scatter | solution.py:302
  1884.1 153.2 %all-reduce.19.cloned.1.call-done = (bf16[1024,2048]{1,0:T(8,128)(2,1)}, bf16[1024,2048]{1,0:T(8,128)(2,1)}) async-done(((bf16[1024,2048]{1,0:T(8,128)(2,1)}, bf16[1024,2048]{1,0:T(8,128)(2,1)}), (bf16[1024,2048]{1,0:T(8,128)(2,1)}, bf16[1024,2048]{1,0:T(8,128)(2,1)})) %all-reduce.19.cloned.1.call-update) | async-done | bytes 8388624 | tf_op jit(solution)/shard_map/psum | solution.py:200
  2037.4 7.3 fusion.106
  2044.7 22.3 %all-reduce.8 = (bf16[2048]{0:T(1024)(128)(2,1)S(1)}, bf16[256]{0:T(256)(128)(2,1)S(1)}, bf16[512]{0:T(512)(128)(2,1)S(1)}, bf16[2048]{0:T(1024)(128)(2,1)S(1)}) all-reduce(bf16[2048]{0:T(1024)(128)(2,1)S(1)} %get-tuple-element.836, bf16[256]{0:T(256)(128)(2,1)S(1)} %get-tuple-element.934, ...), channel_id=4, replica_groups=mesh['dp'=8,'tensor'=4] {'dp'}, use_global_device_ids=true, to_apply=%region_35.36.clone | all-reduce | flops 4864 | bytes 19456
  2067.1 6.2 psum.48
  2075.7 33.1 %reduce-scatter.17.cloned.1.call-done = bf16[256,512]{1,0:T(8,128)(2,1)} async-done(((bf16[2048,512]{1,0:T(8,128)(2,1)}), bf16[256,512]{1,0:T(8,128)(2,1)}) %reduce-scatter.17.cloned.1.call-update) | async-done | bytes 262160 | tf_op jit(solution)/shard_map/reduce_scatter | solution.py:305
  2110.6 18.2 fusion.105
  (1229 shorter events, 705.3 us)
Async XLA Ops:
  7.2 59.6 %copy-start.45 = (u32[32]{0:T(128)S(1)}, u32[32]{0:T(128)}, u32[]{:S(2)}) copy-start(u32[32]{0:T(128)} %constant.208) | copy-start | bytes 388
  7.2 29.0 %copy-start.43 = (bf16[256,16]{0,1:T(8,128)(2,1)S(1)}, bf16[256,16]{0,1:T(8,128)(2,1)}, u32[]{:S(2)}) copy-start(bf16[256,16]{0,1:T(8,128)(2,1)} %param.35) | copy-start | bytes 24580
  7.2 61.5 %copy-start.51 = (bf16[64]{0:T(256)(128)(2,1)S(1)}, bf16[64]{0:T(256)(128)(2,1)}, u32[]{:S(2)}) copy-start(bf16[64]{0:T(256)(128)(2,1)} %param.38) | copy-start | bytes 388
  7.2 61.7 %copy-start.52 = (bf16[32]{0:T(256)(128)(2,1)S(1)}, bf16[32]{0:T(256)(128)(2,1)}, u32[]{:S(2)}) copy-start(bf16[32]{0:T(256)(128)(2,1)} %param.37) | copy-start | bytes 196
  7.2 79.4 %copy-start.44 = (bf16[16,32]{1,0:T(8,128)(2,1)S(1)}, bf16[16,32]{1,0:T(8,128)(2,1)}, u32[]{:S(2)}) copy-start(bf16[16,32]{1,0:T(8,128)(2,1)} %param.36) | copy-start | bytes 3076
  7.2 121.6 %all-gather.16.cloned.1.call-start = ((), (), s32[]{:S(2)}) async-start(), calls=%async_computation.10 | async-start | bytes 1179648 | tf_op jit(solution)/shard_map/all_gather | solution.py:130
  8.0 127.7 %all-gather.20.cloned.1.call-start = ((), (), s32[]{:S(2)}) async-start(), calls=%async_computation.12 | async-start | bytes 1179648 | tf_op jit(solution)/shard_map/all_gather | solution.py:129
  8.7 136.1 %all-gather.18.cloned.1.call-start = ((), (), s32[]{:S(2)}) async-start(), calls=%async_computation.11 | async-start | bytes 2359296 | tf_op jit(solution)/shard_map/all_gather | solution.py:131
  9.5 310.8 %all-gather.22.cloned.1.call-start = ((), (), s32[]{:S(2)}) async-start(), calls=%async_computation.13 | async-start | bytes 2359296 | tf_op jit(solution)/shard_map/all_gather | solution.py:132
  10.0 359.6 %all-gather.32.cloned.1.call-start = ((), (), s32[]{:S(2)}) async-start(), calls=%async_computation.29 | async-start | bytes 4718592 | tf_op jit(solution)/shard_map/all_gather | solution.py:18
  33.0 87.7 %copy-start.34 = (f32[8,1,256]{2,1,0:T(1,128)}, f32[8,1,256]{2,1,0:T(1,128)S(1)}, u32[]{:S(2)}) copy-start(f32[8,1,256]{2,1,0:T(1,128)S(1)} %convert_element_type.291) | copy-start | bytes 24580
  36.2 84.6 %copy-start.38 = (f32[1024]{0:T(1024)}, f32[1024]{0:T(1024)S(1)}, u32[]{:S(2)}) copy-start(f32[1024]{0:T(1024)S(1)} %add_rsqrt_fusion.2) | copy-start | bytes 12292
  66.8 54.0 %copy-start.32 = (bf16[2048,16]{0,1:T(8,128)(2,1)}, bf16[2048,16]{0,1:T(8,128)(2,1)S(1)}, u32[]{:S(2)}) copy-start(bf16[2048,16]{0,1:T(8,128)(2,1)S(1)} %all_gather.59) | copy-start | bytes 196612
  297.5 123.4 %all-gather.24.cloned.1.call-start = ((), (), s32[]{:S(2)}) async-start(), calls=%async_computation.14 | async-start | bytes 2359296 | tf_op jit(solution)/shard_map/all_gather | solution.py:137
  298.1 281.7 %all-reduce.15.cloned.1.call-start = ((), (), s32[]{:S(2)}) async-start(), calls=%async_computation.15 | async-start | bytes 16777216 | tf_op jit(solution)/shard_map/psum | solution.py:190
  300.4 26.4 %copy-start.12 = (f32[256,1,8,128]{0,3,2,1:T(8,128)}, f32[256,1,8,128]{0,3,2,1:T(8,128)S(1)}, u32[]{:S(2)}) copy-start(f32[256,1,8,128]{0,3,2,1:T(8,128)S(1)} %copy.147) | copy-start | bytes 3145732
  300.4 26.4 %copy-start.36 = (f32[1024]{0:T(1024)}, f32[1024]{0:T(1024)S(1)}, u32[]{:S(2)}) copy-start(f32[1024]{0:T(1024)S(1)} %compare_convert_fusion.5) | copy-start | bytes 12292
  378.1 7.7 copy-start.6
  428.6 246.2 %all-gather.26.cloned.1.call-start = ((), (), s32[]{:S(2)}) async-start(), calls=%async_computation.16 | async-start | bytes 6488064 | tf_op jit(solution)/shard_map/all_gather | solution.py:141
  429.4 338.5 %all-gather.28.cloned.1.call-start = ((), (), s32[]{:S(2)}) async-start(), calls=%async_computation.17 | async-start | bytes 6488064 | tf_op jit(solution)/shard_map/all_gather | solution.py:142
  430.1 431.4 %all-gather.30.cloned.1.call-start = ((), (), s32[]{:S(2)}) async-start(), calls=%async_computation.18 | async-start | bytes 6488064 | tf_op jit(solution)/shard_map/all_gather | solution.py:143
  430.7 617.7 %all-reduce.17.cloned.1.call-start = ((), (), s32[]{:S(2)}) async-start(), calls=%async_computation.19 | async-start | bytes 16777216 | tf_op jit(solution)/shard_map/psum | solution.py:214
  579.8 8.2 copy-start.1
  877.2 10.9 copy-start.57
  877.2 10.9 copy-start.56
  877.2 10.9 copy-start.47
  897.2 377.1 %all-gather.34.cloned.1.call-start = ((), (), s32[]{:S(2)}) async-start(), calls=%async_computation.30 | async-start | bytes 4718592 | tf_op jit(solution)/shard_map/all_gather | solution.py:18
  1048.4 8.2 copy-start.5
  1068.5 7.5 copy-start.28
  1075.5 7.6 copy-start.24
  1075.5 557.6 %reduce-scatter.23.cloned.1.call-start = ((), (), s32[]{:S(2)}) async-start(), calls=%async_computation.25 | async-start | bytes 2359296 | tf_op jit(solution)/shard_map/reduce_scatter | solution.py:323
  1083.1 551.9 %reduce-scatter.19.cloned.1.call-start = ((), (), s32[]{:S(2)}) async-start(), calls=%async_computation.23 | async-start | bytes 2359296 | tf_op jit(solution)/shard_map/reduce_scatter | solution.py:308
  1089.3 547.5 %reduce-scatter.25.cloned.1.call-start = ((), (), s32[]{:S(2)}) async-start(), calls=%async_computation.26 | async-start | bytes 6488064 | tf_op jit(solution)/shard_map/reduce_scatter | solution.py:329
  1100.4 538.7 %reduce-scatter.27.cloned.1.call-start = ((), (), s32[]{:S(2)}) async-start(), calls=%async_computation.27 | async-start | bytes 6488064 | tf_op jit(solution)/shard_map/reduce_scatter | solution.py:332
  1112.7 528.7 %reduce-scatter.29.cloned.1.call-start = ((), (), s32[]{:S(2)}) async-start(), calls=%async_computation.28 | async-start | bytes 6488064 | tf_op jit(solution)/shard_map/reduce_scatter | solution.py:335
  1265.3 428.8 %reduce-scatter.31.cloned.1.call-start = ((), (), s32[]{:S(2)}) async-start(), calls=%async_computation.31 | async-start | bytes 73728
  1289.9 265.1 %copy-start.37 = (f32[1024]{0:T(1024)S(1)}, f32[1024]{0:T(1024)}, u32[]{:S(2)}) copy-start(f32[1024]{0:T(1024)} %copy-done.36) | copy-start | bytes 12292
  1563.6 16.6 copy-start.19
  1576.6 173.9 %reduce-scatter.21.cloned.1.call-start = ((), (), s32[]{:S(2)}) async-start(), calls=%async_computation.24 | async-start | bytes 73728 | tf_op jit(solution)/shard_map/reduce_scatter | solution.py:311
  1580.1 236.2 %reduce-scatter.13.cloned.1.call-start = ((), (), s32[]{:S(2)}) async-start(), calls=%async_computation.20 | async-start | bytes 1179648 | tf_op jit(solution)/shard_map/reduce_scatter | solution.py:299
  1584.7 11.2 copy-start.25
  1584.7 297.8 %reduce-scatter.15.cloned.1.call-start = ((), (), s32[]{:S(2)}) async-start(), calls=%async_computation.21 | async-start | bytes 1179648 | tf_op jit(solution)/shard_map/reduce_scatter | solution.py:302
  1584.8 11.2 copy-start.49
  1604.1 433.3 %all-reduce.19.cloned.1.call-start = ((), (), s32[]{:S(2)}) async-start(), calls=%async_computation.32 | async-start | bytes 16777216 | tf_op jit(solution)/shard_map/psum | solution.py:200
  1621.5 487.3 %reduce-scatter.17.cloned.1.call-start = ((), (), s32[]{:S(2)}) async-start(), calls=%async_computation.22 | async-start | bytes 2359296 | tf_op jit(solution)/shard_map/reduce_scatter | solution.py:305
  1634.9 402.5 %copy-start.33 = (bf16[2048,16]{0,1:T(8,128)(2,1)S(1)}, bf16[2048,16]{0,1:T(8,128)(2,1)}, u32[]{:S(2)}) copy-start(bf16[2048,16]{0,1:T(8,128)(2,1)} %copy-done.32) | copy-start | bytes 196612
  1634.9 402.5 %copy-start.35 = (f32[8,1,256]{2,1,0:T(1,128)S(1)}, f32[8,1,256]{2,1,0:T(1,128)}, u32[]{:S(2)}) copy-start(f32[8,1,256]{2,1,0:T(1,128)} %copy-done.34) | copy-start | bytes 24580
  1634.9 402.5 %copy-start.39 = (f32[1024]{0:T(1024)S(1)}, f32[1024]{0:T(1024)}, u32[]{:S(2)}) copy-start(f32[1024]{0:T(1024)} %copy-done.38) | copy-start | bytes 12292
  (33 other events, 105.5 us)
Sparse Core Ops, SparseCore 0:
  10.2 42.9 all-gather.15
  55.3 39.1 all-gather.19
  96.7 48.0 all-gather.17
  146.8 47.8 all-gather.21
  297.7 71.9 all-gather.31
  371.5 49.3 all-gather.23
  428.7 151.0 all-reduce.14
  582.0 92.7 all-gather.25
  677.0 90.8 all-gather.27
  769.7 91.7 all-gather.29
  897.3 151.0 all-reduce.16
  1075.6 73.5 all-gather.33
  1152.7 66.4 reduce-scatter.22
  1222.6 66.8 reduce-scatter.18
  1293.0 108.9 reduce-scatter.24
  1405.5 109.7 reduce-scatter.26
  1518.8 110.3 reduce-scatter.28
  1633.0 61.0 reduce-scatter.30
  1697.8 52.6 reduce-scatter.20
  1753.8 62.5 reduce-scatter.12
  1820.1 62.3 reduce-scatter.14
  1885.1 152.2 all-reduce.18
  2040.9 67.8 reduce-scatter.16
where the time goes:
time: 2150 us; the launch traced here: 2140 us
  waiting for transfers between devices  1030 us (48%)
  matrix products  337 us (16%)
  other arithmetic  301 us (14%)
  local copies, waits for them, and re-layouts  252 us (12%)
  blocking collectives  177 us (8%)
    psum x1, waiting for transfers between devices, shards(): lax.psum(ffn_part.astype(jnp.bfloat16), 'tensor').astype(jnp.float32)  153 us
    psum x1, waiting for transfers between devices, shards(): d_normed_two = lax.psum(d_normed_part, 'tensor')  151 us
    psum x1, waiting for transfers between devices, shards(): branch = lax.psum(branch_part, 'tensor')  131 us
    dynamic_slice x144, local copies, waits for them, and re-layouts, own_part(): finished, outputs = lax.scan(jax.checkpoint(group_step), initial, inputs)  92.3 us
    all_gather x1, waiting for transfers between devices, shards(): lax.all_gather(w_down, 'dp', axis=1, tiled=True)  82 us
    all_gather x1, waiting for transfers between devices, shards(): lax.all_gather(w_up, 'dp', axis=0, tiled=True)  81.3 us
    all_gather x1, waiting for transfers between devices, shards(): lax.all_gather(w_gate, 'dp', axis=0, tiled=True)  80.7 us
    reduce_scatter x1, waiting for transfers between devices, shards(): lax.psum_scatter(grad_key.astype(jnp.bfloat16), 'dp', scatter_dimension=0...  64.5 us
  transfers between devices with their start and end apart: 23, of which 14 were waited for; matrix products, arithmetic and copies ran while one was open for 37% of the time, Pallas kernels for 0%

commit v1 on v0

v1 whole, which is shorter than its diff:
```python
import functools

import jax
import jax.numpy as jnp
from jax import lax
from jax.experimental import pallas as pl
from jax.experimental.pallas import tpu as pltpu
from jax.sharding import PartitionSpec as P

DK = 256
DV = 512
RANK = 16
BLOCK = 128
SMALL = 128
EPSILON = 1e-06
GATE_NORMALIZER = 16.0
HIGHEST = lax.Precision.HIGHEST
F32 = jnp.float32
BF16 = jnp.bfloat16
NN = ((1,), (0,))
NT = ((1,), (1,))
TN = ((0,), (0,))
VMEM_BYTES = 50 * 1024 * 1024


def low_dot(left, right, dims):
    return lax.dot_general(
        left.astype(BF16), right.astype(BF16), (dims, ((), ())), preferred_element_type=F32
    )


class Ring:
    def __init__(self, axis, depth=2):
        self.axis, self.depth = axis, depth
        self.n = lax.axis_size(axis)
        n = self.n
        order = list(range(0, n, 2)) + list(range(n - 1, 0, -2))
        self.nexts = [(order[i], order[(i + 1) % n]) for i in range(n)]
        self.prevs = [(order[i], order[(i - 1) % n]) for i in range(n)]
        me = lax.axis_index(axis)
        self.place = jnp.where(me % 2 == 0, me // 2, n - 1 - me // 2)
        self.sent = ([], [])

    def at(self, offset):
        place = (self.place + offset + self.n) % self.n
        return jnp.where(place < self.n // 2, 2 * place, 2 * (self.n - place) - 1)

    def send(self, value, backward):
        past = self.sent[backward]
        if len(past) >= self.depth:
            value, _ = lax.optimization_barrier((value, past[-self.depth]))
        arrived = lax.ppermute(value, self.axis, self.prevs if backward else self.nexts)
        past.append(arrived)
        return arrived

    def gather(self, parts, dims):
        n = self.n

        def put(whole, piece, block, dim, extra=0):
            start = [0, 0]
            start[dim] = block * part_size[dim] + (extra if dim == 0 else 0)
            if dim == 1:
                start[0] = extra
            return lax.dynamic_update_slice(whole, piece, start)

        wholes = []
        for part, dim in zip(parts, dims):
            part_size = part.shape
            shape = list(part.shape)
            shape[dim] *= n
            wholes.append(put(jnp.zeros(shape, part.dtype), part, self.at(0), dim))
        ahead, behind = list(parts), list(parts)
        for step in range(1, n // 2):
            for i, dim in enumerate(dims):
                part_size = parts[i].shape
                ahead[i] = self.send(ahead[i], 0)
                behind[i] = self.send(behind[i], 1)
                wholes[i] = put(wholes[i], ahead[i], self.at(-step), dim)
                wholes[i] = put(wholes[i], behind[i], self.at(step), dim)
        for i, dim in enumerate(dims):
            part_size = parts[i].shape
            half = part_size[0] // 2
            first = self.send(ahead[i][:half], 0)
            second = self.send(behind[i][half:], 1)
            far = self.at(n // 2)
            wholes[i] = put(wholes[i], first, far, dim)
            wholes[i] = put(wholes[i], second, far, dim, half)
        return wholes

    def scatter(self, makers):
        n = self.n
        ahead, behind = [], []
        for maker in makers:
            far = maker(self.at(n // 2)).astype(BF16)
            half = far.shape[0] // 2
            ahead.append(self.send(far[:half], 0))
            behind.append(self.send(far[half:], 1))
        for step in range(n // 2 - 1, 0, -1):
            for i, maker in enumerate(makers):
                front, back = maker(self.at(step)), maker(self.at(-step))
                came, went = ahead[i].astype(F32), behind[i].astype(F32)
                if step == n // 2 - 1:
                    rest = front.shape[0] - came.shape[0]
                    came = jnp.pad(came, ((0, rest), (0, 0)))
                    went = jnp.pad(went, ((front.shape[0] - went.shape[0], 0), (0, 0)))
                ahead[i] = self.send((front + came).astype(BF16), 0)
                behind[i] = self.send((back + went).astype(BF16), 1)
        return [
            maker(self.at(0)) + ahead[i].astype(F32) + behind[i].astype(F32)
            for i, maker in enumerate(makers)
        ]


def swap(value, distance):
    return lax.ppermute(value, "tensor", [(i, i ^ distance) for i in range(4)])


def tensor_place():
    mine = lax.axis_index("tensor")
    return mine % 2, mine // 2


def tensor_scatter(partial):
    core, side = tensor_place()
    half = partial.shape[0] // 2
    quarter = half // 2
    other = swap(lax.dynamic_slice_in_dim(partial, (1 - core) * half, half, 0), 1)
    pair = lax.dynamic_slice_in_dim(partial, core * half, half, 0).astype(F32) + other.astype(F32)
    across = swap(lax.dynamic_slice_in_dim(pair, (1 - side) * quarter, quarter, 0).astype(BF16), 2)
    return lax.dynamic_slice_in_dim(pair, side * quarter, quarter, 0) + across.astype(F32)


def ordered(mine, other, first):
    return jnp.concatenate(
        [jnp.where(first, mine, other), jnp.where(first, other, mine)], axis=0
    )


def tensor_gather(quarter):
    core, side = tensor_place()
    half = ordered(quarter, swap(quarter, 2), side == 0)
    return ordered(half, swap(half, 1), core == 0)


def tensor_sum(value):
    value = value + swap(value, 1)
    return value + swap(value, 2)


def quarter_of(value):
    core, side = tensor_place()
    quarter = value.shape[0] // 4
    return lax.dynamic_slice_in_dim(value, (core * 2 + side) * quarter, quarter, 0)


def chain_states(decay, state, backward):
    n = lax.axis_size("dp")

    def shifted(value, distance):
        pairs = [(i, i + distance) for i in range(n - distance)]
        if backward:
            pairs = [(b, a) for a, b in pairs]
        return lax.ppermute(value, "dp", pairs)

    def pack(decay, state):
        return jnp.concatenate([state, jnp.broadcast_to(decay, (16, DK))], axis=0).astype(BF16)

    def unpack(packed):
        packed = packed.astype(F32)
        return packed[DV : DV + 1], packed[:DV]

    decay, state = unpack(shifted(pack(decay, state), 1))
    distance = 1
    while distance < n - 1:
        more_decay, more_state = unpack(shifted(pack(decay, state), distance))
        decay, state = decay * more_decay, decay * more_state + state
        distance *= 2
    return state


def segments(info_ref, places):
    total = jnp.zeros_like(places)
    for j in range(1, info_ref.shape[0]):
        total = total + (info_ref[j] <= places).astype(jnp.int32)
    return total


def block_masks(info_ref, block):
    start = info_ref[0] + block * BLOCK
    rows = lax.broadcasted_iota(jnp.int32, (BLOCK, 1), 0)
    columns = lax.broadcasted_iota(jnp.int32, (1, BLOCK), 1)
    segment = segments(info_ref, start + rows)
    segment_row = segments(info_ref, start + columns)
    allowed = (columns <= rows) & (segment_row == segment)
    previous = segments(info_ref, start - 1)
    last = segments(info_ref, start + BLOCK - 1)
    before = segments(info_ref, info_ref[0] - 1)
    carry = (segment == previous).astype(F32)
    carry_last = (last == previous).astype(F32)
    same_last = (segment == last).astype(F32)
    alive = (segment == before).astype(F32)
    alive_last = (last == before).astype(F32)
    alive_start = (previous == before).astype(F32)
    return allowed, carry, carry_last, same_last, alive, alive_last, alive_start


def triangle(lower, strict):
    rows = lax.broadcasted_iota(jnp.int32, (BLOCK, BLOCK), 0)
    columns = lax.broadcasted_iota(jnp.int32, (BLOCK, BLOCK), 1)
    if not lower:
        rows, columns = columns, rows
    return ((columns < rows) if strict else (columns <= rows)).astype(F32)


def log_decay_of(logit):
    return (jnp.minimum(logit, 0.0) - jnp.log1p(jnp.exp(-jnp.abs(logit)))) / GATE_NORMALIZER


def forward_kernel(
    info_ref, q_ref, k_ref, v_ref, low_ref, up_ref, bias_ref,
    out_ref, reached_ref, logit_ref, scores_ref, states_ref, total_ref, end_ref, reach_ref,
    state, total,
):
    block = pl.program_id(0)

    @pl.when(block == 0)
    def _():
        state[...] = jnp.zeros_like(state)
        total[...] = jnp.zeros_like(total)

    allowed, carry, carry_last, same_last, alive, alive_last, _ = block_masks(info_ref, block)
    q = q_ref[...] * (DK**-0.5)
    k = k_ref[...]
    v = v_ref[...].astype(BF16)
    logit = (
        jnp.dot(low_ref[:, :RANK], up_ref[...], precision=HIGHEST, preferred_element_type=F32)
        + bias_ref[...]
    )
    logit_ref[...] = logit
    decays = jnp.dot(
        triangle(True, False), log_decay_of(logit), precision=HIGHEST, preferred_element_type=F32
    )
    middle = decays[BLOCK // 2 - 1 : BLOCK // 2]
    end = decays[BLOCK - 1 :]
    scores = lax.dot_general(
        q * jnp.exp(decays - middle), k * jnp.exp(middle - decays), (NT, ((), ())),
        precision=HIGHEST, preferred_element_type=F32,
    )
    scores = jnp.where(allowed, scores, 0.0).astype(BF16)
    scores_ref[...] = scores
    held = state[...]
    states_ref[0] = held.astype(BF16)
    total_ref[0] = total[...]
    q_carry = q * jnp.exp(decays) * carry
    out_ref[...] = low_dot(scores, v, NN) + low_dot(q_carry, held, NT)
    k_end = k * jnp.exp(end - decays) * same_last
    state[...] = held * (jnp.exp(end) * carry_last) + low_dot(v, k_end, TN)
    reached_ref[...] = (q * jnp.exp(decays + total[...]) * alive).astype(BF16)
    total[...] = total[...] + end

    @pl.when(block == pl.num_programs(0) - 1)
    def _():
        end_ref[...] = state[...]
        reach_ref[...] = jnp.exp(total[...]) * alive_last


def forward_states(info, mixer, up_rank, bias):
    count = mixer.shape[0]
    blocks = count // BLOCK
    at_block = lambda i, info: (i, 0)
    fixed = lambda i, info: (0, 0)
    return pl.pallas_call(
        forward_kernel,
        grid_spec=pltpu.PrefetchScalarGridSpec(
            num_scalar_prefetch=1,
            grid=(blocks,),
            in_specs=[
                pl.BlockSpec((BLOCK, DK), lambda i, info: (i, 0)),
                pl.BlockSpec((BLOCK, DK), lambda i, info: (i, 1)),
                pl.BlockSpec((BLOCK, DV), lambda i, info: (i, 1)),
                pl.BlockSpec((BLOCK, SMALL), lambda i, info: (i, (2 * DK + DV) // SMALL)),
                pl.BlockSpec((RANK, DK), fixed),
                pl.BlockSpec((1, DK), fixed),
            ],
            out_specs=[
                pl.BlockSpec((BLOCK, DV), at_block),
                pl.BlockSpec((BLOCK, DK), at_block),
                pl.BlockSpec((BLOCK, DK), at_block),
                pl.BlockSpec((BLOCK, BLOCK), at_block),
                pl.BlockSpec((1, DV, DK), lambda i, info: (i, 0, 0)),
                pl.BlockSpec((1, 1, DK), lambda i, info: (i, 0, 0)),
                pl.BlockSpec((DV, DK), fixed),
                pl.BlockSpec((1, DK), fixed),
            ],
            scratch_shapes=[pltpu.VMEM((DV, DK), F32), pltpu.VMEM((1, DK), F32)],
        ),
        out_shape=[
            jax.ShapeDtypeStruct((count, DV), F32),
            jax.ShapeDtypeStruct((count, DK), BF16),
            jax.ShapeDtypeStruct((count, DK), F32),
            jax.ShapeDtypeStruct((count, BLOCK), BF16),
            jax.ShapeDtypeStruct((blocks, DV, DK), BF16),
            jax.ShapeDtypeStruct((blocks, 1, DK), F32),
            jax.ShapeDtypeStruct((DV, DK), F32),
            jax.ShapeDtypeStruct((1, DK), F32),
        ],
        compiler_params=pltpu.CompilerParams(vmem_limit_bytes=VMEM_BYTES),
        cost_estimate=pl.CostEstimate(flops=10**10, bytes_accessed=2 * 10**7, transcendentals=10**6),
        name="forward_states",
    )(info, mixer, mixer, mixer, mixer, up_rank, bias)


def backward_kernel(
    info_ref, q_ref, k_ref, v_ref, low_ref, logit_ref, scores_ref, states_ref, total_ref, grad_ref,
    up_ref, incoming_ref, later_ref,
    out_ref, up_grad_ref, bias_grad_ref,
    adjoint,
):
    step = pl.program_id(0)
    block = pl.num_programs(0) - 1 - step

    @pl.when(step == 0)
    def _():
        adjoint[...] = later_ref[...]
        up_grad_ref[...] = jnp.zeros_like(up_grad_ref)
        bias_grad_ref[...] = jnp.zeros_like(bias_grad_ref)

    allowed, carry, carry_last, same_last, _, _, alive_start = block_masks(info_ref, block)
    q = q_ref[...] * (DK**-0.5)
    k = k_ref[...]
    v = v_ref[...].astype(BF16)
    grad_exact = grad_ref[...]
    grad = grad_exact.astype(BF16)
    grad_rest = (grad_exact - grad.astype(F32)).astype(BF16)
    logit = logit_ref[...]
    decays = jnp.dot(
        triangle(True, False), log_decay_of(logit), precision=HIGHEST, preferred_element_type=F32
    )
    middle = decays[BLOCK // 2 - 1 : BLOCK // 2]
    end = decays[BLOCK - 1 :]
    q_factor = jnp.exp(decays - middle)
    k_factor = jnp.exp(middle - decays)
    carry_factor = jnp.exp(decays) * carry
    end_factor = jnp.exp(end - decays) * same_last
    q_low = (q * q_factor).astype(BF16)
    k_low = (k * k_factor).astype(BF16)
    q_carry = (q * carry_factor).astype(BF16)
    k_end = (k * end_factor).astype(BF16)
    held = states_ref[0].astype(F32) + incoming_ref[...] * (jnp.exp(total_ref[0]) * alive_start)
    after = adjoint[...]
    held_low = held.astype(BF16)
    after_low = after.astype(BF16)
    scores = scores_ref[...]
    d_scores = low_dot(grad, v, NT) + low_dot(grad_rest, v, NT)
    d_scores = jnp.where(allowed, d_scores, 0.0).astype(BF16)
    d_q_low = low_dot(d_scores, k_low, NN)
    d_k_low = low_dot(d_scores, q_low, TN)
    d_v = low_dot(scores, grad, TN) + low_dot(k_end, after_low, NT)
    d_q_carry = low_dot(grad, held_low, NN)
    d_k_end = low_dot(v, after_low, NN)
    d_q = d_q_low * q_factor + d_q_carry * carry_factor
    d_k = d_k_low * k_factor + d_k_end * end_factor
    later_part = (
        d_q_low * q_low.astype(F32)
        - d_k_low * k_low.astype(F32)
        + d_q_carry * q_carry.astype(F32)
    )
    earlier_part = d_k_end * k_end.astype(F32)
    through = jnp.exp(end) * carry_last
    state_part = through * jnp.sum(after * held, axis=0, keepdims=True)
    d_decay = (
        jnp.dot(triangle(False, False), later_part, precision=HIGHEST, preferred_element_type=F32)
        + jnp.dot(triangle(True, True), earlier_part, precision=HIGHEST, preferred_element_type=F32)
        + state_part
    )
    adjoint[...] = after * through + low_dot(grad, q_carry, TN)
    d_logit = d_decay * jax.nn.sigmoid(-logit) * (1.0 / GATE_NORMALIZER)
    low = low_ref[:, :RANK]
    up_grad_ref[...] += lax.dot_general(
        low, d_logit, (TN, ((), ())), precision=HIGHEST, preferred_element_type=F32
    )
    bias_grad_ref[...] += jnp.sum(d_logit, axis=0, keepdims=True)
    d_low = lax.dot_general(
        d_logit, up_ref[...], (NT, ((), ())), precision=HIGHEST, preferred_element_type=F32
    )
    out_ref[:, :DK] = (d_q * (DK**-0.5)).astype(BF16)
    out_ref[:, DK : 2 * DK] = d_k.astype(BF16)
    out_ref[:, 2 * DK : 2 * DK + DV] = d_v.astype(BF16)
    out_ref[:, 2 * DK + DV :] = d_low.astype(BF16)


def backward_states(info, mixer, logit, scores, states, total, grad, up_rank, incoming, later):
    count = mixer.shape[0]
    blocks = count // BLOCK
    width = mixer.shape[1]
    up_wide = jnp.pad(up_rank, ((0, SMALL - RANK), (0, 0)))
    fixed = lambda i, info: (0, 0)
    turned = lambda column: (lambda i, info: (blocks - 1 - i, column))
    turned3 = lambda i, info: (blocks - 1 - i, 0, 0)
    return pl.pallas_call(
        backward_kernel,
        grid_spec=pltpu.PrefetchScalarGridSpec(
            num_scalar_prefetch=1,
            grid=(blocks,),
            in_specs=[
                pl.BlockSpec((BLOCK, DK), turned(0)),
                pl.BlockSpec((BLOCK, DK), turned(1)),
                pl.BlockSpec((BLOCK, DV), turned(1)),
                pl.BlockSpec((BLOCK, SMALL), turned((2 * DK + DV) // SMALL)),
                pl.BlockSpec((BLOCK, DK), turned(0)),
                pl.BlockSpec((BLOCK, BLOCK), turned(0)),
                pl.BlockSpec((1, DV, DK), turned3),
                pl.BlockSpec((1, 1, DK), turned3),
                pl.BlockSpec((BLOCK, DV), turned(0)),
                pl.BlockSpec((SMALL, DK), fixed),
                pl.BlockSpec((DV, DK), fixed),
                pl.BlockSpec((DV, DK), fixed),
            ],
            out_specs=[
                pl.BlockSpec((BLOCK, width), turned(0)),
                pl.BlockSpec((RANK, DK), fixed),
                pl.BlockSpec((1, DK), fixed),
            ],
            scratch_shapes=[pltpu.VMEM((DV, DK), F32)],
        ),
        out_shape=[
            jax.ShapeDtypeStruct((count, width), BF16),
            jax.ShapeDtypeStruct((RANK, DK), F32),
            jax.ShapeDtypeStruct((1, DK), F32),
        ],
        compiler_params=pltpu.CompilerParams(vmem_limit_bytes=VMEM_BYTES),
        cost_estimate=pl.CostEstimate(flops=2 * 10**10, bytes_accessed=2 * 10**7, transcendentals=10**6),
        name="backward_states",
    )(info, mixer, mixer, mixer, mixer, logit, scores, states, total, grad, up_wide, incoming, later)


def head_parts(mixed, outgate, gain):
    inverse = lax.rsqrt(jnp.mean(mixed * mixed, axis=-1, keepdims=True) + EPSILON)
    unit = mixed * inverse
    return inverse, unit, unit * gain, jax.nn.sigmoid(outgate)


def mix_kernel(within_ref, reached_ref, incoming_ref, outgate_ref, gain_ref, weight_ref,
               mixed_ref, gated_ref, branch_ref):
    mixed = within_ref[...] + low_dot(reached_ref[...], incoming_ref[...], NT)
    mixed_ref[...] = mixed
    outgate = outgate_ref[...]
    _, _, head_out, sigmoid = head_parts(mixed, outgate, gain_ref[...])
    gated = (head_out * (outgate * sigmoid)).astype(BF16)
    gated_ref[...] = gated
    branch_ref[...] = low_dot(gated, weight_ref[...], NN).astype(BF16)


def mix(within, reached, incoming, outgate, gain, weight):
    count, width = within.shape[0], weight.shape[1]
    rows = min(256, count)
    at_block = lambda i: (i, 0)
    fixed = lambda i: (0, 0)
    return pl.pallas_call(
        mix_kernel,
        grid=(count // rows,),
        in_specs=[
            pl.BlockSpec((rows, DV), at_block),
            pl.BlockSpec((rows, DK), at_block),
            pl.BlockSpec((DV, DK), fixed),
            pl.BlockSpec((rows, DV), at_block),
            pl.BlockSpec((1, DV), fixed),
            pl.BlockSpec((DV, width), fixed),
        ],
        out_specs=[
            pl.BlockSpec((rows, DV), at_block),
            pl.BlockSpec((rows, DV), at_block),
            pl.BlockSpec((rows, width), at_block),
        ],
        out_shape=[
            jax.ShapeDtypeStruct((count, DV), F32),
            jax.ShapeDtypeStruct((count, DV), BF16),
            jax.ShapeDtypeStruct((count, width), BF16),
        ],
        compiler_params=pltpu.CompilerParams(vmem_limit_bytes=VMEM_BYTES),
        cost_estimate=pl.CostEstimate(flops=6 * 10**9, bytes_accessed=2 * 10**7, transcendentals=10**6),
        name="mix",
    )(within, reached, incoming, outgate, gain, weight)


def unmix_kernel(grad_ref, weight_ref, mixed_ref, outgate_ref, gain_ref, reached_ref,
                 d_mixed_ref, d_outgate_ref, gain_grad_ref, own_ref):
    @pl.when(pl.program_id(0) == 0)
    def _():
        gain_grad_ref[...] = jnp.zeros_like(gain_grad_ref)
        own_ref[...] = jnp.zeros_like(own_ref)

    d_gated = low_dot(grad_ref[...], weight_ref[...], NT)
    outgate = outgate_ref[...]
    gain = gain_ref[...]
    inverse, unit, head_out, sigmoid = head_parts(mixed_ref[...], outgate, gain)
    d_head_out = d_gated * (outgate * sigmoid)
    d_outgate = d_gated * head_out * sigmoid * (1.0 + outgate * (1.0 - sigmoid))
    d_outgate_ref[...] = d_outgate.astype(BF16)
    gain_grad_ref[...] += jnp.sum(d_head_out * unit, axis=0, keepdims=True)
    scaled = d_head_out * gain
    d_mixed = inverse * (scaled - unit * jnp.mean(scaled * unit, axis=-1, keepdims=True))
    d_mixed_ref[...] = d_mixed
    own_ref[...] += low_dot(d_mixed, reached_ref[...], TN)


def unmix(grad, weight, mixed, outgate, gain, reached):
    count, width = grad.shape
    rows = min(256, count)
    at_block = lambda i: (i, 0)
    fixed = lambda i: (0, 0)
    return pl.pallas_call(
        unmix_kernel,
        grid=(count // rows,),
        in_specs=[
            pl.BlockSpec((rows, width), at_block),
            pl.BlockSpec((DV, width), fixed),
            pl.BlockSpec((rows, DV), at_block),
            pl.BlockSpec((rows, DV), at_block),
            pl.BlockSpec((1, DV), fixed),
            pl.BlockSpec((rows, DK), at_block),
        ],
        out_specs=[
            pl.BlockSpec((rows, DV), at_block),
            pl.BlockSpec((rows, DV), at_block),
            pl.BlockSpec((1, DV), fixed),
            pl.BlockSpec((DV, DK), fixed),
        ],
        out_shape=[
            jax.ShapeDtypeStruct((count, DV), F32),
            jax.ShapeDtypeStruct((count, DV), BF16),
            jax.ShapeDtypeStruct((1, DV), F32),
            jax.ShapeDtypeStruct((DV, DK), F32),
        ],
        compiler_params=pltpu.CompilerParams(vmem_limit_bytes=VMEM_BYTES),
        cost_estimate=pl.CostEstimate(flops=6 * 10**9, bytes_accessed=2 * 10**7, transcendentals=10**6),
        name="unmix",
    )(grad, weight, mixed, outgate, gain, reached)


def rms_inverse(values):
    return lax.rsqrt(jnp.mean(values * values, axis=-1, keepdims=True) + EPSILON)


def norm_back(d_normed, gains, unit, inverse):
    scaled = d_normed * gains
    return inverse * (scaled - unit * jnp.mean(scaled * unit, axis=-1, keepdims=True))


def product(left, right):
    return jnp.dot(left, right, preferred_element_type=F32)


def shards(
    tokens, out_grad, starts, attn_gain, w_query, w_key, w_value, w_outgate, w_decay_down,
    w_decay_up, decay_bias, head_gain, w_output, ffn_gain, w_gate, w_up, w_down,
):
    ring = Ring("dp")
    n = ring.n
    rows = w_query.shape[0]
    ranks, heads = w_decay_up.shape[1], head_gain.shape[0]

    side = jnp.zeros((rows, SMALL), BF16)
    side = side.at[:, :RANK].set(w_decay_down)
    side = side.at[:, RANK].set(attn_gain)
    side = side.at[:, RANK + 1].set(ffn_gain)
    side = side.at[:RANK, 32 : 32 + ranks].set(w_decay_up)
    side = side.at[RANK, 32 : 32 + ranks].set(decay_bias)
    side = side.at[RANK + 1, 32 : 32 + heads].set(head_gain)
    mixer_part = jnp.concatenate([w_query, w_key, w_value, side], axis=1)
    width = mixer_part.shape[1]
    half = rows // 2
    halves = ring.gather([mixer_part[:half], mixer_part[half:]], [0, 0])
    full_mixer = jnp.concatenate(
        [h.reshape(n, half, width) for h in halves], axis=1
    ).reshape(n * rows, width)
    full_outgate, full_output = ring.gather([w_outgate, w_output], [0, 1])
    full_gate, full_up = ring.gather([w_gate, w_up], [0, 0])
    (full_down,) = ring.gather([w_down], [1])

    full_side = full_mixer[:, width - SMALL :]
    gain_one = full_side[:, RANK].astype(F32)
    gain_two = full_side[:, RANK + 1].astype(F32)
    blocks = full_side.reshape(n, rows, SMALL)
    up_rank = (
        blocks[:, :RANK, 32 : 32 + ranks].transpose(1, 0, 2).reshape(RANK, n * ranks).astype(F32)
    )
    bias = blocks[:, RANK, 32 : 32 + ranks].reshape(1, n * ranks).astype(F32)
    head_gains = blocks[:, RANK + 1, 32 : 32 + heads].reshape(1, n * heads).astype(F32)

    count = tokens.shape[0]
    info = jnp.concatenate([(lax.axis_index("dp") * count)[None].astype(jnp.int32), starts])

    inputs = tokens.astype(F32)
    normed = (inputs * rms_inverse(inputs) * gain_one).astype(BF16)
    mixer = product(normed, full_mixer)
    within, reached, logit, scores, states, total, end, reach = forward_states(
        info, mixer, up_rank, bias
    )
    incoming = chain_states(reach, end, False)
    outgate = product(normed, full_outgate)
    mixed, gated, branch_part = mix(within, reached, incoming, outgate, head_gains, full_output)
    hidden_in = quarter_of(inputs) + tensor_scatter(branch_part)

    inverse_two = rms_inverse(hidden_in)
    unit_two = hidden_in * inverse_two
    normed_two = tensor_gather((unit_two * gain_two).astype(BF16))
    gate_pre = product(normed_two, full_gate)
    up_proj = product(normed_two, full_up)
    gate_sigmoid = jax.nn.sigmoid(gate_pre)
    gate_silu = gate_pre * gate_sigmoid
    hidden = (gate_silu * up_proj).astype(BF16)
    ffn_out = tensor_scatter(product(hidden, full_down).astype(BF16))
    output = tensor_gather((hidden_in + ffn_out).astype(BF16))

    d_hidden = jnp.einsum("td,fd->tf", out_grad, full_down, preferred_element_type=F32)
    d_gate = (d_hidden * up_proj * gate_sigmoid * (1.0 + gate_pre * (1.0 - gate_sigmoid))).astype(
        BF16
    )
    d_up = (d_hidden * gate_silu).astype(BF16)
    d_normed_part = jnp.einsum("tf,df->td", d_gate, full_gate, preferred_element_type=F32)
    d_normed_part = d_normed_part + jnp.einsum(
        "tf,df->td", d_up, full_up, preferred_element_type=F32
    )
    d_normed_two = tensor_scatter(d_normed_part.astype(BF16))

    def columns_of(value, d):
        return lax.dynamic_slice_in_dim(value, d * rows, rows, 1)

    def rows_maker(left, right):
        return lambda d: jnp.einsum(
            "tr,tc->rc", columns_of(left, d), right, preferred_element_type=F32
        )

    def columns_maker(left, right):
        return lambda d: jnp.einsum(
            "tr,tc->rc", left, columns_of(right, d), preferred_element_type=F32
        )

    (sum_down,) = ring.scatter([columns_maker(hidden, out_grad)])
    sum_gate, sum_up = ring.scatter([rows_maker(normed_two, d_gate), rows_maker(normed_two, d_up)])

    d_hidden_in = quarter_of(out_grad).astype(F32) + norm_back(
        d_normed_two, gain_two, unit_two, inverse_two
    )
    d_branch = tensor_gather(d_hidden_in.astype(BF16))

    d_mixed, d_outgate, grad_head_gain, own = unmix(
        d_branch, full_output, mixed, outgate, head_gains, reached
    )
    later = chain_states(reach, own, True)
    sum_output, sum_outgate = ring.scatter(
        [columns_maker(gated, d_branch), rows_maker(normed, d_outgate)]
    )
    d_mixer, grad_up_rank, grad_bias = backward_states(
        info, mixer, logit, scores, states, total, d_mixed, up_rank, incoming, later
    )
    d_first = jnp.einsum("tk,dk->td", d_mixer, full_mixer, preferred_element_type=F32)
    d_first = d_first + jnp.einsum(
        "tk,dk->td", d_outgate, full_outgate, preferred_element_type=F32
    )
    d_normed = tensor_scatter(d_first.astype(BF16))

    packed = jnp.zeros((n, rows, SMALL), F32)
    packed = packed.at[:, :RANK, 32 : 32 + ranks].set(
        grad_up_rank.reshape(RANK, n, ranks).transpose(1, 0, 2)
    )
    packed = packed.at[:, RANK, 32 : 32 + ranks].set(grad_bias.reshape(n, ranks))
    packed = packed.at[:, RANK + 1, 32 : 32 + heads].set(grad_head_gain.reshape(n, heads))
    packed = packed.reshape(n * rows, SMALL)

    def mixer_maker(upper):
        def maker(d):
            columns = lax.dynamic_slice_in_dim(normed, d * rows + (0 if upper else half), half, 1)
            chunk = jnp.einsum("tr,tc->rc", columns, d_mixer, preferred_element_type=F32)
            extra = lax.dynamic_slice_in_dim(packed, d * rows + (0 if upper else half), half, 0)
            return chunk + jnp.pad(extra, ((0, 0), (width - SMALL, 0)))

        return maker

    sum_mixer = jnp.concatenate(ring.scatter([mixer_maker(True), mixer_maker(False)]), axis=0)
    sum_query, sum_key = sum_mixer[:, :DK], sum_mixer[:, DK : 2 * DK]
    sum_value = sum_mixer[:, 2 * DK : 2 * DK + DV]
    sum_side = sum_mixer[:, 2 * DK + DV :]

    own_inputs = quarter_of(inputs)
    inverse_one = rms_inverse(own_inputs)
    input_grad = tensor_gather(
        (
            d_hidden_in + norm_back(d_normed, gain_one, own_inputs * inverse_one, inverse_one)
        ).astype(BF16)
    ).astype(F32)

    def weighted(pairs):
        return sum(jnp.sum(w.astype(F32) * g, axis=1, keepdims=True) for w, g in pairs)

    attn_part = weighted(
        [
            (w_query, sum_query),
            (w_key, sum_key),
            (w_value, sum_value),
            (w_outgate, sum_outgate),
            (w_decay_down, sum_side[:, :RANK]),
        ]
    )
    ffn_part = weighted([(w_gate, sum_gate), (w_up, sum_up)])
    shared = tensor_sum(jnp.concatenate([sum_side[:, :RANK], attn_part, ffn_part], axis=1))
    return (
        output,
        input_grad,
        shared[:, RANK] / attn_gain.astype(F32),
        sum_query,
        sum_key,
        sum_value,
        sum_outgate,
        shared[:, :RANK],
        sum_side[:RANK, 32 : 32 + ranks],
        sum_side[RANK, 32 : 32 + ranks],
        sum_side[RANK + 1, 32 : 32 + heads],
        sum_output,
        shared[:, RANK + 1] / ffn_gain.astype(F32),
        sum_gate,
        sum_up,
        sum_down,
    )


def solution(mesh):
    return jax.shard_map(
        shards,
        mesh=mesh,
        in_specs=(
            P("dp", None),
            P("dp", None),
            P(),
            P("dp"),
            P("dp", "tensor"),
            P("dp", "tensor"),
            P("dp", "tensor"),
            P("dp", "tensor"),
            P("dp", None),
            P(None, ("tensor", "dp")),
            P(("tensor", "dp")),
            P(("tensor", "dp")),
            P("tensor", "dp"),
            P("dp"),
            P("dp", "tensor"),
            P("dp", "tensor"),
            P("tensor", "dp"),
        ),
        out_specs=(
            P("dp", None),
            P("dp", None),
            P("dp"),
            P("dp", "tensor"),
            P("dp", "tensor"),
            P("dp", "tensor"),
            P("dp", "tensor"),
            P("dp", None),
            P(None, ("tensor", "dp")),
            P(("tensor", "dp")),
            P(("tensor", "dp")),
            P("tensor", "dp"),
            P("dp"),
            P("dp", "tensor"),
            P("dp", "tensor"),
            P("tensor", "dp"),
        ),
        check_vma=False,
    )
```

time: 2150 us -> 836 us (0.39)
  waiting for transfers between devices: 1030 us -> 248 us
  other arithmetic: 301 us -> 67.5 us
  starting transfers between devices: 1.97 us -> 213 us
  blocking collectives: 177 us -> 0 us
  matrix products: 337 us -> 161 us
  local copies, waits for them, and re-layouts: 252 us -> 87.4 us
  Pallas kernels: 0 us -> 47.7 us
    psum x3 -> x0, waiting for transfers between devices: 436 us -> none  [the longest x1 153 us: shards(): lax.psum(ffn_part.astype(jnp.bfloat16), 'tensor').astype(jnp.float32)]
    all_gather x10 -> x0, waiting for transfers between devices: 323 us -> none  [the longest x1 82 us: shards(): lax.all_gather(w_down, 'dp', axis=1, tiled=True)]
    ppermute x0 -> x138, waiting for transfers between devices: none -> 248 us  [the longest x112 198 us: send(): lax.ppermute(value, self.axis, self.prevs if backward else self.nexts)]
    reduce_scatter x9 -> x0, waiting for transfers between devices: 217 us -> none  [the longest x1 64.5 us: shards(): lax.psum_scatter(grad_key.astype(jnp.bfloat16), 'dp', scatter_dimension=0...]
    ppermute x0 -> x138, starting transfers between devices: none -> 213 us  [the longest x112 178 us: send(): lax.ppermute(value, self.axis, self.prevs if backward else self.nexts)]
    dot_general x257 -> x66, matrix products: 337 us -> 161 us  [the longest x5 46.5 us: product(): return jnp.dot(left, right, preferred_element_type=F32)]
    all_gather x5 -> x0, blocking collectives: 120 us -> none  [the longest x1 30.9 us: shards(): lax.all_gather(w_decay_up, 'dp', axis=1, tiled=True)]
    dynamic_slice x158 -> x5, local copies, waits for them, and re-layouts: 92.4 us -> 5.46 us  [the longest x4 5.33 us: tensor_scatter(): lax.dynamic_slice_in_dim(partial, (1 - core) * half, half, 0)]
  transfers between devices with their start and end apart: 23 -> 138, of which waited for: 14 -> 50; matrix products, arithmetic and copies ran while one was open for 37% -> 27% of each run, Pallas kernels for 0% -> 4%
where the time goes in v1:
time: 836 us; the launch traced here: 827 us
  waiting for transfers between devices  248 us (30%)
  starting transfers between devices  213 us (25%)
  matrix products  161 us (19%)
  local copies, waits for them, and re-layouts  87.4 us (10%)
  other arithmetic  67.5 us (8%)
  Pallas kernels  47.7 us (6%)
    ppermute x112, waiting for transfers between devices, send(): lax.ppermute(value, self.axis, self.prevs if backward else self.nexts)  198 us
    ppermute x112, starting transfers between devices, send(): lax.ppermute(value, self.axis, self.prevs if backward else self.nexts)  178 us
    dot_general x5, matrix products, product(): return jnp.dot(left, right, preferred_element_type=F32)  46.5 us
    dynamic_update_slice x62, local copies, waits for them, and re-layouts, put(): return lax.dynamic_update_slice(whole, piece, start)  43.1 us
    ppermute x18, waiting for transfers between devices, swap(): return lax.ppermute(value, 'tensor', [(i, i ^ distance) for i in range(4)])  36.9 us
    dot_general x24, matrix products, rows_maker(): jnp.einsum('tr,tc->rc', columns_of(left, d), right, preferred_element_typ...  33.2 us
    dot_general x16, matrix products, columns_maker(): jnp.einsum('tr,tc->rc', left, columns_of(right, d), preferred_element_typ...  22.9 us
    ppermute x8, starting transfers between devices, shifted(): return lax.ppermute(value, 'dp', pairs)  21.3 us
  transfers between devices with their start and end apart: 138, of which 50 were waited for; matrix products, arithmetic and copies ran while one was open for 27% of the time, Pallas kernels for 4%

profile of v1, /device:TPU:0, one launch (start us, length us, event | category | flops | bytes accessed | tf_op | source)
XLA Modules:
  0.0 827.1 jit_solution(527244607969562361)
XLA Ops:
  40.8 6.7 convert_element_type.512
  61.5 4.2 collective-permute-done.2
  74.3 4.1 collective-permute-done.4
  96.5 7.2 fusion.212.q_ref.k_ref.v_ref.low_ref
  104.0 13.7 %forward_states.1 = (f32[1024,512]{1,0:T(8,128)}, bf16[1024,256]{1,0:T(8,128)(2,1)S(1)}, f32[1024,256]{1,0:T(8,128)S(1)}, bf16[1024,128]{1,0:T(8,128)(2,1)S(1)},...) custom-call(s32[6]{0:T(128)S(1)} %pad_add_fusion.info_ref, ...), custom_call_target="tpu_custom_call" | custom-call | flops 10000000000 | bytes 20000000 | tf_op jit(solution)/shard_map/forward_states/pallas_call | solution.py:272
  144.4 5.4 collective-permute-start.18
  166.3 4.1 collective-permute-start.49
  171.7 5.4 fusion.213.outgate_ref
  180.6 7.8 mix.1
  196.4 10.0 %collective-permute-start.42 = (bf16[256,1408]{1,0:T(8,128)(2,1)S(1)}, bf16[256,1408]{1,0:T(8,128)(2,1)S(1)}, u32[]{:S(2)}, u32[]{:S(2)}) collective-permute-start(bf16[256,1408]{1,0:T(8,128)(2,1)S(1)} %collective-permute-done.40), channel_id=1, source_target_pairs={{0,8},{8,16},{16,24},{24,28},{28,20},{20,12},{12,4},{4,0},{1,9},{9... | collective-permute-start | bytes 2162696 | tf_op jit(solution)/shard_map/ppermute | solution.py:52
  211.9 10.0 %collective-permute-start.52 = (bf16[256,1408]{1,0:T(8,128)(2,1)S(1)}, bf16[256,1408]{1,0:T(8,128)(2,1)S(1)}, u32[]{:S(2)}, u32[]{:S(2)}) collective-permute-start(bf16[256,1408]{1,0:T(8,128)(2,1)S(1)} %collective-permute-done.50), channel_id=1, source_target_pairs={{0,8},{8,16},{16,24},{24,28},{28,20},{20,12},{12,4},{4,0},{1,9},{9... | collective-permute-start | bytes 2162696 | tf_op jit(solution)/shard_map/ppermute | solution.py:52
  223.1 4.2 collective-permute-done.42
  227.3 10.0 %collective-permute-start.44 = (bf16[256,1408]{1,0:T(8,128)(2,1)S(1)}, bf16[256,1408]{1,0:T(8,128)(2,1)S(1)}, u32[]{:S(2)}, u32[]{:S(2)}) collective-permute-start(bf16[256,1408]{1,0:T(8,128)(2,1)S(1)} %collective-permute-done.42), channel_id=1, source_target_pairs={{0,8},{8,16},{16,24},{24,28},{28,20},{20,12},{12,4},{4,0},{1,9},{9... | collective-permute-start | bytes 2162696 | tf_op jit(solution)/shard_map/ppermute | solution.py:52
  242.8 10.1 %collective-permute-start.54 = (bf16[128,1408]{1,0:T(8,128)(2,1)S(1)}, bf16[128,1408]{1,0:T(8,128)(2,1)S(1)}, u32[]{:S(2)}, u32[]{:S(2)}) collective-permute-start(bf16[128,1408]{1,0:T(8,128)(2,1)S(1)} %slice.482), channel_id=1, source_target_pairs={{0,8},{8,16},{16,24},{24,28},{28,20},{20,12},{12,4},{4,0},{1,9},{9... | collective-permute-start | bytes 1081352 | tf_op jit(solution)/shard_map/ppermute | solution.py:52
  254.1 4.2 collective-permute-done.44
  258.2 10.1 %collective-permute-start.46 = (bf16[128,1408]{1,0:T(8,128)(2,1)S(1)}, bf16[128,1408]{1,0:T(8,128)(2,1)S(1)}, u32[]{:S(2)}, u32[]{:S(2)}) collective-permute-start(bf16[128,1408]{1,0:T(8,128)(2,1)S(1)} %slice.480), channel_id=1, source_target_pairs={{0,8},{8,16},{16,24},{24,28},{28,20},{20,12},{12,4},{4,0},{1,9},{9... | collective-permute-start | bytes 1081352 | tf_op jit(solution)/shard_map/ppermute | solution.py:52
  274.0 6.3 collective-permute-done.47
  284.0 12.6 %collective-permute-done.57 = bf16[1408,256]{1,0:T(8,128)(2,1)S(1)} collective-permute-done((bf16[1408,256]{1,0:T(8,128)(2,1)S(1)}, bf16[1408,256]{1,0:T(8,128)(2,1)S(1)}, u32[]{:S(2)}, u32[]{:S(2)}) %collective-permute-start.57) | collective-permute-done | bytes 720928 | tf_op jit(solution)/shard_map/ppermute | solution.py:52
  305.8 11.7 %collective-permute-done.59 = bf16[1408,256]{1,0:T(8,128)(2,1)S(1)} collective-permute-done((bf16[1408,256]{1,0:T(8,128)(2,1)S(1)}, bf16[1408,256]{1,0:T(8,128)(2,1)S(1)}, u32[]{:S(2)}, u32[]{:S(2)}) %collective-permute-start.59) | collective-permute-done | bytes 720928 | tf_op jit(solution)/shard_map/ppermute | solution.py:52
  321.1 11.6 %collective-permute-done.61 = bf16[1408,256]{1,0:T(8,128)(2,1)S(1)} collective-permute-done((bf16[1408,256]{1,0:T(8,128)(2,1)S(1)}, bf16[1408,256]{1,0:T(8,128)(2,1)S(1)}, u32[]{:S(2)}, u32[]{:S(2)}) %collective-permute-start.61) | collective-permute-done | bytes 720928 | tf_op jit(solution)/shard_map/ppermute | solution.py:52
  335.3 5.2 collective-permute-done.62
  340.6 8.5 %fusion.214 = f32[1408,1024]{0,1:T(8,128)} fusion(bf16[1408,2048]{1,0:T(8,128)(2,1)S(1)} %constant_dynamic-update-slice_fusion.61, bf16[1024,2048]{1,0:T(8,128)(2,1)S(1)} %copy-done.44), kind=kOutput, calls=%fused_computation.466 | convolution fusion | flops 5905580032 | bytes 15728640 | tf_op jit(solution)/shard_map/td,fd->tf/dot_general | solution.py:616
  350.6 9.6 %fusion.8 = f32[1024,1408]{1,0:T(8,128)} fusion(bf16[2048,1408]{1,0:T(8,128)(2,1)S(1)} %constant_dynamic-update-slice_fusion.17, bf16[512,2048]{1,0:T(8,128)(2,1)S(1)} %get-tuple-element.437, bf16[512,2048]{1,0:T(8,128)(2,1)S(1)} %get-tuple-element.436), kind=kOutput, calls=%fused_computation.72 | convolution fusion | flops 5913968640 | bytes 15728640 | tf_op jit(solution)/shard_map/dot_general | solution.py:551
  360.2 15.4 %fusion.2 = (bf16[1024,1408]{1,0:T(8,128)(2,1)S(1)}, bf16[1024,1408]{1,0:T(8,128)(2,1)S(1)}, bf16[1024,1408]{1,0:T(8,128)(2,1)}) fusion(f32[1408,1024]{0,1:T(8,128)} %fusion.214, f32[1024,1408]{1,0:T(8,128)} %fusion.8, bf16[2048,1408]{1,0:T(8,128)(2,1)} %constant_dynamic-update-slice_fusion.8, bf16[512,2048]{1,0:T(8,128)(2,1)S(1)} %get-tuple-element.437, ...), kind=kOutput, calls=%fused_computation.42 | convolution fusion | flops 5935595520 | bytes 30146560 | tf_op jit(solution)/shard_map/dot_general | solution.py:551
  378.6 8.9 %convolution_convert_fusion = bf16[1024,2048]{1,0:T(8,128)(2,1)S(1)} fusion(bf16[1024,1408]{1,0:T(8,128)(2,1)S(1)} %copy-done.57, bf16[1408,2048]{1,0:T(8,128)(2,1)} %copy-done.21), kind=kOutput, calls=%fused_computation.54 | convolution fusion | flops 5907677184 | bytes 12845056 | tf_op jit(solution)/shard_map/dot_general | solution.py:551
  387.5 12.3 %fusion.215 = f32[1024,2048]{1,0:T(8,128)} fusion(bf16[1024,1408]{1,0:T(8,128)(2,1)S(1)} %get-tuple-element.427, bf16[2048,1408]{1,0:T(8,128)(2,1)} %constant_dynamic-update-slice_fusion.8), kind=kOutput, calls=%fused_computation.467 | convolution fusion | flops 5905580032 | bytes 17039360 | tf_op jit(solution)/shard_map/tf,df->td/dot_general | solution.py:622
  406.6 10.5 %add_convert_fusion.1 = bf16[1024,2048]{1,0:T(8,128)(2,1)} fusion(f32[1024,2048]{1,0:T(8,128)} %fusion.215, bf16[1024,1408]{1,0:T(8,128)(2,1)S(1)} %get-tuple-element.426, bf16[2048,1408]{1,0:T(8,128)(2,1)S(1)} %bitcast.123), kind=kOutput, calls=%fused_computation.35 | convolution fusion | flops 5909774336 | bytes 21233664 | tf_op jit(solution)/shard_map/tf,df->td/dot_general | solution.py:621
  425.8 14.9 %collective-permute-done.81 = bf16[1408,256]{1,0:T(8,128)(2,1)S(1)} collective-permute-done((bf16[1408,256]{1,0:T(8,128)(2,1)S(1)}, bf16[1408,256]{1,0:T(8,128)(2,1)S(1)}, u32[]{:S(2)}, u32[]{:S(2)}) %collective-permute-start.81) | collective-permute-done | bytes 720928 | tf_op jit(solution)/shard_map/ppermute | solution.py:52
  446.2 13.4 %collective-permute-done.82 = bf16[1408,256]{1,0:T(8,128)(2,1)S(1)} collective-permute-done((bf16[1408,256]{1,0:T(8,128)(2,1)S(1)}, bf16[1408,256]{1,0:T(8,128)(2,1)S(1)}, u32[]{:S(2)}, u32[]{:S(2)}) %collective-permute-start.82) | collective-permute-done | bytes 720928 | tf_op jit(solution)/shard_map/ppermute | solution.py:52
  472.5 13.2 %collective-permute-done.83 = bf16[128,1408]{1,0:T(8,128)(2,1)S(1)} collective-permute-done((bf16[128,1408]{1,0:T(8,128)(2,1)S(1)}, bf16[128,1408]{1,0:T(8,128)(2,1)S(1)}, u32[]{:S(2)}, u32[]{:S(2)}) %collective-permute-start.83) | collective-permute-done | bytes 360480 | tf_op jit(solution)/shard_map/ppermute | solution.py:52
  497.0 10.6 %collective-permute-done.84 = bf16[256,1408]{1,0:T(8,128)(2,1)S(1)} collective-permute-done((bf16[256,1408]{1,0:T(8,128)(2,1)S(1)}, bf16[256,1408]{1,0:T(8,128)(2,1)S(1)}, u32[]{:S(2)}, u32[]{:S(2)}) %collective-permute-start.84) | collective-permute-done | bytes 720928 | tf_op jit(solution)/shard_map/ppermute | solution.py:52
  538.6 7.7 collective-permute-done.112
  555.4 17.9 %collective-permute-done.113 = bf16[256,1408]{1,0:T(8,128)(2,1)S(1)} collective-permute-done((bf16[256,1408]{1,0:T(8,128)(2,1)S(1)}, bf16[256,1408]{1,0:T(8,128)(2,1)S(1)}, u32[]{:S(2)}, u32[]{:S(2)}) %collective-permute-start.113) | collective-permute-done | bytes 720928 | tf_op jit(solution)/shard_map/ppermute | solution.py:52
  583.4 9.6 %collective-permute-done.114 = bf16[256,1408]{1,0:T(8,128)(2,1)S(1)} collective-permute-done((bf16[256,1408]{1,0:T(8,128)(2,1)S(1)}, bf16[256,1408]{1,0:T(8,128)(2,1)S(1)}, u32[]{:S(2)}, u32[]{:S(2)}) %collective-permute-start.114) | collective-permute-done | bytes 720928 | tf_op jit(solution)/shard_map/ppermute | solution.py:52
  605.0 8.4 %unmix.1 = (f32[1024,512]{1,0:T(8,128)}, bf16[1024,512]{1,0:T(8,128)(2,1)S(1)}, f32[1,512]{1,0:T(1,128)S(1)}, f32[512,256]{1,0:T(8,128)S(1)}) custom-call(bf16[1024,2048]{1,0:T(8,128)(2,1)} %pad_maximum_fusion.1.grad_ref, bf16[512,2048]{1,0:T(8,128)(2,1)} %constant_dynamic-update-slice_fusion.62.weight_ref, f32[1024,512]{1,0:T(8,128)} %get-tuple-element.311.mixed_ref, ...), custom_call_target="tpu_custom_call" | custom-call | flops 6000000000 | bytes 20000000 | tf_op jit(solution)/shard_map/unmix/pallas_call | solution.py:512
  620.4 7.3 fusion.216
  650.1 4.0 collective-permute-start.89
  660.1 4.1 collective-permute-done.89
  672.9 4.1 collective-permute-done.74
  678.9 7.4 collective-permute-done.131
  689.5 8.4 %collective-permute-done.75 = bf16[528,256]{1,0:T(8,128)(2,1)S(1)} collective-permute-done((bf16[528,256]{1,0:T(8,128)(2,1)S(1)}, bf16[528,256]{1,0:T(8,128)(2,1)S(1)}, u32[]{:S(2)}, u32[]{:S(2)}) %collective-permute-start.75) | collective-permute-done | bytes 270368 | tf_op jit(solution)/shard_map/ppermute | solution.py:163
  698.0 17.8 %backward_states.1 = (bf16[1024,1152]{1,0:T(8,128)(2,1)}, f32[16,256]{1,0:T(8,128)S(1)}, f32[1,256]{1,0:T(1,128)S(1)}) custom-call(s32[6]{0:T(128)S(1)} %copy-done.5, f32[1024,1152]{1,0:T(8,128)} %fusion.212.q_ref.k_ref.v_ref.low_ref, f32[1024,1152]{1,0:T(8,128)} %fusion.212.q_ref.k_ref.v_ref.low_ref, f32[1024,1152]{1,0:T(8,128)} %fusion.212.q_ref.k_ref.v_ref.low_ref, ...), custom_call_target="tpu_custom_call" | custom-call | flops 20000000000 | bytes 20000000 | tf_op jit(solution)/shard_map/backward_states/pallas_call | solution.py:400
  717.6 4.2 scatter.40
  732.3 9.5 %add_convert_fusion = bf16[1024,2048]{1,0:T(8,128)(2,1)S(1)} fusion(f32[1024,2048]{1,0:T(8,128)} %fusion.216, bf16[1024,1152]{1,0:T(8,128)(2,1)S(1)} %copy-done.8, bf16[2048,1152]{1,0:T(8,128)(2,1)} %bitcast.119), kind=kOutput, calls=%fused_computation.34 | convolution fusion | flops 4836032512 | bytes 19660800 | tf_op jit(solution)/shard_map/tk,dk->td/dot_general | solution.py:658
  748.6 3.9 collective-permute-done.92
  774.8 12.1 %collective-permute-done.77 = bf16[256,2048]{1,0:T(8,128)(2,1)S(1)} collective-permute-done((bf16[256,2048]{1,0:T(8,128)(2,1)S(1)}, bf16[256,2048]{1,0:T(8,128)(2,1)S(1)}, u32[]{:S(2)}, u32[]{:S(2)}) %collective-permute-start.77) | collective-permute-done | bytes 1048608 | tf_op jit(solution)/shard_map/ppermute | solution.py:115
  790.1 21.0 %collective-permute-done.78 = bf16[256,2048]{1,0:T(8,128)(2,1)S(1)} collective-permute-done((bf16[256,2048]{1,0:T(8,128)(2,1)S(1)}, bf16[256,2048]{1,0:T(8,128)(2,1)S(1)}, u32[]{:S(2)}, u32[]{:S(2)}) %collective-permute-start.78) | collective-permute-done | bytes 1048608 | tf_op jit(solution)/shard_map/ppermute | solution.py:115
  822.7 4.3 maximum_convert_fusion
  (675 shorter events, 390.3 us)
Async XLA Ops:
  18.5 30.9 %collective-permute-start.8 = (bf16[128,1152]{1,0:T(8,128)(2,1)S(1)}, bf16[128,1152]{1,0:T(8,128)(2,1)S(1)}, u32[]{:S(2)}, u32[]{:S(2)}) collective-permute-start(bf16[128,1152]{1,0:T(8,128)(2,1)S(1)} %get-tuple-element.473), channel_id=1, source_target_pairs={{0,8},{8,16},{16,24},{24,28},{28,20},{20,12},{12,4},{4,0},{1,9},{9... | collective-permute-start | bytes 884744 | tf_op jit(solution)/shard_map/ppermute | solution.py:52
  21.5 30.0 %collective-permute-start.9 = (bf16[128,1152]{1,0:T(8,128)(2,1)S(1)}, bf16[128,1152]{1,0:T(8,128)(2,1)S(1)}, u32[]{:S(2)}, u32[]{:S(2)}) collective-permute-start(bf16[128,1152]{1,0:T(8,128)(2,1)S(1)} %get-tuple-element.473), channel_id=1, source_target_pairs={{0,4},{8,0},{16,8},{24,16},{28,24},{20,28},{12,20},{4,12},{1,5},{9... | collective-permute-start | bytes 884744 | tf_op jit(solution)/shard_map/ppermute | solution.py:52
  21.5 30.0 %collective-permute-start = (bf16[128,1152]{1,0:T(8,128)(2,1)S(1)}, bf16[128,1152]{1,0:T(8,128)(2,1)S(1)}, u32[]{:S(2)}, u32[]{:S(2)}) collective-permute-start(bf16[128,1152]{1,0:T(8,128)(2,1)S(1)} %get-tuple-element.471), channel_id=1, source_target_pairs={{0,8},{8,16},{16,24},{24,28},{28,20},{20,12},{12,4},{4,0},{1,9},{9... | collective-permute-start | bytes 884744 | tf_op jit(solution)/shard_map/ppermute | solution.py:52
  23.6 30.0 %collective-permute-start.1 = (bf16[128,1152]{1,0:T(8,128)(2,1)S(1)}, bf16[128,1152]{1,0:T(8,128)(2,1)S(1)}, u32[]{:S(2)}, u32[]{:S(2)}) collective-permute-start(bf16[128,1152]{1,0:T(8,128)(2,1)S(1)} %get-tuple-element.471), channel_id=1, source_target_pairs={{0,4},{8,0},{16,8},{24,16},{28,24},{20,28},{12,20},{4,12},{1,5},{9... | collective-permute-start | bytes 884744 | tf_op jit(solution)/shard_map/ppermute | solution.py:52
  90.9 31.0 %collective-permute-start.28 = (bf16[512,256]{1,0:T(8,128)(2,1)}, bf16[512,256]{1,0:T(8,128)(2,1)}, u32[]{:S(2)}, u32[]{:S(2)}) collective-permute-start(bf16[512,256]{1,0:T(8,128)(2,1)} %param.47), channel_id=1, source_target_pairs={{0,8},{8,16},{16,24},{24,28},{28,20},{20,12},{12,4},{4,0},{1,9},{9... | collective-permute-start | bytes 786440 | tf_op jit(solution)/shard_map/ppermute | solution.py:52
  92.6 30.9 %collective-permute-start.29 = (bf16[512,256]{1,0:T(8,128)(2,1)}, bf16[512,256]{1,0:T(8,128)(2,1)}, u32[]{:S(2)}, u32[]{:S(2)}) collective-permute-start(bf16[512,256]{1,0:T(8,128)(2,1)} %param.47), channel_id=1, source_target_pairs={{0,4},{8,0},{16,8},{24,16},{28,24},{20,28},{12,20},{4,12},{1,5},{9... | collective-permute-start | bytes 786440 | tf_op jit(solution)/shard_map/ppermute | solution.py:52
  93.0 31.0 %collective-permute-start.20 = (bf16[256,512]{1,0:T(8,128)(2,1)S(1)}, bf16[256,512]{1,0:T(8,128)(2,1)}, u32[]{:S(2)}, u32[]{:S(2)}) collective-permute-start(bf16[256,512]{1,0:T(8,128)(2,1)S(1)} %copy-done.36), channel_id=1, source_target_pairs={{0,8},{8,16},{16,24},{24,28},{28,20},{20,12},{12,4},{4,0},{1,9},{9... | collective-permute-start | bytes 786440 | tf_op jit(solution)/shard_map/ppermute | solution.py:52
  94.6 30.9 %collective-permute-start.21 = (bf16[256,512]{1,0:T(8,128)(2,1)S(1)}, bf16[256,512]{1,0:T(8,128)(2,1)}, u32[]{:S(2)}, u32[]{:S(2)}) collective-permute-start(bf16[256,512]{1,0:T(8,128)(2,1)S(1)} %copy-done.36), channel_id=1, source_target_pairs={{0,4},{8,0},{16,8},{24,16},{28,24},{20,28},{12,20},{4,12},{1,5},{9... | collective-permute-start | bytes 786440 | tf_op jit(solution)/shard_map/ppermute | solution.py:52
  163.8 26.5 %collective-permute-start.48 = (bf16[256,1408]{1,0:T(8,128)(2,1)S(1)}, bf16[256,1408]{1,0:T(8,128)(2,1)S(1)}, u32[]{:S(2)}, u32[]{:S(2)}) collective-permute-start(bf16[256,1408]{1,0:T(8,128)(2,1)S(1)} %copy-done.33), channel_id=1, source_target_pairs={{0,8},{8,16},{16,24},{24,28},{28,20},{20,12},{12,4},{4,0},{1,9},{9... | collective-permute-start | bytes 2162696 | tf_op jit(solution)/shard_map/ppermute | solution.py:52
  166.3 24.7 %collective-permute-start.49 = (bf16[256,1408]{1,0:T(8,128)(2,1)S(1)}, bf16[256,1408]{1,0:T(8,128)(2,1)S(1)}, u32[]{:S(2)}, u32[]{:S(2)}) collective-permute-start(bf16[256,1408]{1,0:T(8,128)(2,1)S(1)} %copy-done.33), channel_id=1, source_target_pairs={{0,4},{8,0},{16,8},{24,16},{28,24},{20,28},{12,20},{4,12},{1,5},{9... | collective-permute-start | bytes 2162696 | tf_op jit(solution)/shard_map/ppermute | solution.py:52
  177.1 29.3 %collective-permute-start.41 = (bf16[256,1408]{1,0:T(8,128)(2,1)S(1)}, bf16[256,1408]{1,0:T(8,128)(2,1)S(1)}, u32[]{:S(2)}, u32[]{:S(2)}) collective-permute-start(bf16[256,1408]{1,0:T(8,128)(2,1)S(1)} %copy-done.30), channel_id=1, source_target_pairs={{0,4},{8,0},{16,8},{24,16},{28,24},{20,28},{12,20},{4,12},{1,5},{9... | collective-permute-start | bytes 2162696 | tf_op jit(solution)/shard_map/ppermute | solution.py:52
  190.2 81.1 %collective-permute-start.36 = (bf16[512,2048]{1,0:T(8,128)(2,1)S(1)}, bf16[512,2048]{1,0:T(8,128)(2,1)S(1)}, u32[]{:S(2)}, u32[]{:S(2)}) collective-permute-start(bf16[512,2048]{1,0:T(8,128)(2,1)S(1)} %constant_dynamic-slice_fusion.19), channel_id=1, source_target_pairs={{0,1},{1,0},{2,3},{3,2},{4,5},{5,4},{6,7},{7,6},{8,9},{9,8},{10,11... | collective-permute-start | bytes 6291464 | tf_op jit(solution)/shard_map/ppermute | solution.py:115
  191.0 30.9 %collective-permute-start.51 = (bf16[256,1408]{1,0:T(8,128)(2,1)S(1)}, bf16[256,1408]{1,0:T(8,128)(2,1)S(1)}, u32[]{:S(2)}, u32[]{:S(2)}) collective-permute-start(bf16[256,1408]{1,0:T(8,128)(2,1)S(1)} %collective-permute-done.49), channel_id=1, source_target_pairs={{0,4},{8,0},{16,8},{24,16},{28,24},{20,28},{12,20},{4,12},{1,5},{9... | collective-permute-start | bytes 2162696 | tf_op jit(solution)/shard_map/ppermute | solution.py:52
  196.4 30.9 %collective-permute-start.42 = (bf16[256,1408]{1,0:T(8,128)(2,1)S(1)}, bf16[256,1408]{1,0:T(8,128)(2,1)S(1)}, u32[]{:S(2)}, u32[]{:S(2)}) collective-permute-start(bf16[256,1408]{1,0:T(8,128)(2,1)S(1)} %collective-permute-done.40), channel_id=1, source_target_pairs={{0,8},{8,16},{16,24},{24,28},{28,20},{20,12},{12,4},{4,0},{1,9},{9... | collective-permute-start | bytes 2162696 | tf_op jit(solution)/shard_map/ppermute | solution.py:52
  206.4 30.9 %collective-permute-start.43 = (bf16[256,1408]{1,0:T(8,128)(2,1)S(1)}, bf16[256,1408]{1,0:T(8,128)(2,1)S(1)}, u32[]{:S(2)}, u32[]{:S(2)}) collective-permute-start(bf16[256,1408]{1,0:T(8,128)(2,1)S(1)} %collective-permute-done.41), channel_id=1, source_target_pairs={{0,4},{8,0},{16,8},{24,16},{28,24},{20,28},{12,20},{4,12},{1,5},{9... | collective-permute-start | bytes 2162696 | tf_op jit(solution)/shard_map/ppermute | solution.py:52
  211.9 30.9 %collective-permute-start.52 = (bf16[256,1408]{1,0:T(8,128)(2,1)S(1)}, bf16[256,1408]{1,0:T(8,128)(2,1)S(1)}, u32[]{:S(2)}, u32[]{:S(2)}) collective-permute-start(bf16[256,1408]{1,0:T(8,128)(2,1)S(1)} %collective-permute-done.50), channel_id=1, source_target_pairs={{0,8},{8,16},{16,24},{24,28},{28,20},{20,12},{12,4},{4,0},{1,9},{9... | collective-permute-start | bytes 2162696 | tf_op jit(solution)/shard_map/ppermute | solution.py:52
  221.9 31.0 %collective-permute-start.53 = (bf16[256,1408]{1,0:T(8,128)(2,1)S(1)}, bf16[256,1408]{1,0:T(8,128)(2,1)S(1)}, u32[]{:S(2)}, u32[]{:S(2)}) collective-permute-start(bf16[256,1408]{1,0:T(8,128)(2,1)S(1)} %collective-permute-done.51), channel_id=1, source_target_pairs={{0,4},{8,0},{16,8},{24,16},{28,24},{20,28},{12,20},{4,12},{1,5},{9... | collective-permute-start | bytes 2162696 | tf_op jit(solution)/shard_map/ppermute | solution.py:52
  227.3 30.9 %collective-permute-start.44 = (bf16[256,1408]{1,0:T(8,128)(2,1)S(1)}, bf16[256,1408]{1,0:T(8,128)(2,1)S(1)}, u32[]{:S(2)}, u32[]{:S(2)}) collective-permute-start(bf16[256,1408]{1,0:T(8,128)(2,1)S(1)} %collective-permute-done.42), channel_id=1, source_target_pairs={{0,8},{8,16},{16,24},{24,28},{28,20},{20,12},{12,4},{4,0},{1,9},{9... | collective-permute-start | bytes 2162696 | tf_op jit(solution)/shard_map/ppermute | solution.py:52
  237.3 31.0 %collective-permute-start.45 = (bf16[256,1408]{1,0:T(8,128)(2,1)S(1)}, bf16[256,1408]{1,0:T(8,128)(2,1)S(1)}, u32[]{:S(2)}, u32[]{:S(2)}) collective-permute-start(bf16[256,1408]{1,0:T(8,128)(2,1)S(1)} %collective-permute-done.43), channel_id=1, source_target_pairs={{0,4},{8,0},{16,8},{24,16},{28,24},{20,28},{12,20},{4,12},{1,5},{9... | collective-permute-start | bytes 2162696 | tf_op jit(solution)/shard_map/ppermute | solution.py:52
  242.8 39.6 %collective-permute-start.54 = (bf16[128,1408]{1,0:T(8,128)(2,1)S(1)}, bf16[128,1408]{1,0:T(8,128)(2,1)S(1)}, u32[]{:S(2)}, u32[]{:S(2)}) collective-permute-start(bf16[128,1408]{1,0:T(8,128)(2,1)S(1)} %slice.482), channel_id=1, source_target_pairs={{0,8},{8,16},{16,24},{24,28},{28,20},{20,12},{12,4},{4,0},{1,9},{9... | collective-permute-start | bytes 1081352 | tf_op jit(solution)/shard_map/ppermute | solution.py:52
  252.9 30.3 %collective-permute-start.55 = (bf16[128,1408]{1,0:T(8,128)(2,1)S(1)}, bf16[128,1408]{1,0:T(8,128)(2,1)S(1)}, u32[]{:S(2)}, u32[]{:S(2)}) collective-permute-start(bf16[128,1408]{1,0:T(8,128)(2,1)S(1)} %slice.483), channel_id=1, source_target_pairs={{0,4},{8,0},{16,8},{24,16},{28,24},{20,28},{12,20},{4,12},{1,5},{9... | collective-permute-start | bytes 1081352 | tf_op jit(solution)/shard_map/ppermute | solution.py:52
  272.2 28.7 %collective-permute-start.37 = (bf16[256,2048]{1,0:T(8,128)(2,1)S(1)}, bf16[256,2048]{1,0:T(8,128)(2,1)S(1)}, u32[]{:S(2)}, u32[]{:S(2)}) collective-permute-start(bf16[256,2048]{1,0:T(8,128)(2,1)S(1)} %dynamic-slice_convert_fusion.3), channel_id=1, source_target_pairs={{0,2},{1,3},{2,0},{3,1},{4,6},{5,7},{6,4},{7,5},{8,10},{9,11},{10,... | collective-permute-start | bytes 3145736 | tf_op jit(solution)/shard_map/ppermute | solution.py:115
  321.0 28.1 %collective-permute-start.39 = (bf16[512,2048]{1,0:T(8,128)(2,1)S(1)}, bf16[512,2048]{1,0:T(8,128)(2,1)S(1)}, u32[]{:S(2)}, u32[]{:S(2)}) collective-permute-start(bf16[512,2048]{1,0:T(8,128)(2,1)S(1)} %pad_maximum_fusion.6), channel_id=1, source_target_pairs={{0,1},{1,0},{2,3},{3,2},{4,5},{5,4},{6,7},{7,6},{8,9},{9,8},{10,11... | collective-permute-start | bytes 6291464 | tf_op jit(solution)/shard_map/ppermute | solution.py:115
  404.5 62.2 %collective-permute-start.64 = (bf16[512,2048]{1,0:T(8,128)(2,1)}, bf16[512,2048]{1,0:T(8,128)(2,1)}, u32[]{:S(2)}, u32[]{:S(2)}) collective-permute-start(bf16[512,2048]{1,0:T(8,128)(2,1)} %constant_dynamic-slice_fusion.18), channel_id=1, source_target_pairs={{0,1},{1,0},{2,3},{3,2},{4,5},{5,4},{6,7},{7,6},{8,9},{9,8},{10,11... | collective-permute-start | bytes 6291464 | tf_op jit(solution)/shard_map/ppermute | solution.py:115
  418.9 51.1 %collective-permute-start.68 = (bf16[512,2048]{1,0:T(8,128)(2,1)S(1)}, bf16[512,2048]{1,0:T(8,128)(2,1)S(1)}, u32[]{:S(2)}, u32[]{:S(2)}) collective-permute-start(bf16[512,2048]{1,0:T(8,128)(2,1)S(1)} %constant_dynamic-slice_fusion.17), channel_id=1, source_target_pairs={{0,1},{1,0},{2,3},{3,2},{4,5},{5,4},{6,7},{7,6},{8,9},{9,8},{10,11... | collective-permute-start | bytes 6291464 | tf_op jit(solution)/shard_map/ppermute | solution.py:115
  461.4 29.9 %collective-permute-start.110 = (bf16[1408,256]{1,0:T(8,128)(2,1)}, bf16[1408,256]{1,0:T(8,128)(2,1)}, u32[]{:S(2)}, u32[]{:S(2)}) collective-permute-start(bf16[1408,256]{1,0:T(8,128)(2,1)} %add_convert_fusion.5), channel_id=1, source_target_pairs={{0,8},{8,16},{16,24},{24,28},{28,20},{20,12},{12,4},{4,0},{1,9},{9... | collective-permute-start | bytes 2162696 | tf_op jit(solution)/shard_map/ppermute | solution.py:52
  464.7 27.0 %collective-permute-start.123 = (bf16[1408,256]{1,0:T(8,128)(2,1)}, bf16[1408,256]{1,0:T(8,128)(2,1)}, u32[]{:S(2)}, u32[]{:S(2)}) collective-permute-start(bf16[1408,256]{1,0:T(8,128)(2,1)} %add_convert_fusion.4), channel_id=1, source_target_pairs={{0,4},{8,0},{16,8},{24,16},{28,24},{20,28},{12,20},{4,12},{1,5},{9... | collective-permute-start | bytes 2162696 | tf_op jit(solution)/shard_map/ppermute | solution.py:52
  470.0 53.7 %collective-permute-start.65 = (bf16[256,2048]{1,0:T(8,128)(2,1)S(1)}, bf16[256,2048]{1,0:T(8,128)(2,1)S(1)}, u32[]{:S(2)}, u32[]{:S(2)}) collective-permute-start(bf16[256,2048]{1,0:T(8,128)(2,1)S(1)} %dynamic-slice_convert_fusion.2), channel_id=1, source_target_pairs={{0,2},{1,3},{2,0},{3,1},{4,6},{5,7},{6,4},{7,5},{8,10},{9,11},{10,... | collective-permute-start | bytes 3145736 | tf_op jit(solution)/shard_map/ppermute | solution.py:115
  485.8 37.0 %collective-permute-start.69 = (bf16[256,2048]{1,0:T(8,128)(2,1)S(1)}, bf16[256,2048]{1,0:T(8,128)(2,1)S(1)}, u32[]{:S(2)}, u32[]{:S(2)}) collective-permute-start(bf16[256,2048]{1,0:T(8,128)(2,1)S(1)} %dynamic-slice_convert_fusion.1), channel_id=1, source_target_pairs={{0,2},{1,3},{2,0},{3,1},{4,6},{5,7},{6,4},{7,5},{8,10},{9,11},{10,... | collective-permute-start | bytes 3145736 | tf_op jit(solution)/shard_map/ppermute | solution.py:115
  491.7 23.7 %collective-permute-start.111 = (bf16[128,1408]{1,0:T(8,128)(2,1)}, bf16[128,1408]{1,0:T(8,128)(2,1)S(1)}, u32[]{:S(2)}, u32[]{:S(2)}) collective-permute-start(bf16[128,1408]{1,0:T(8,128)(2,1)} %get-tuple-element.351), channel_id=1, source_target_pairs={{0,8},{8,16},{16,24},{24,28},{28,20},{20,12},{12,4},{4,0},{1,9},{9... | collective-permute-start | bytes 1081352 | tf_op jit(solution)/shard_map/ppermute | solution.py:52
  519.1 27.2 %collective-permute-start.112 = (bf16[256,1408]{1,0:T(8,128)(2,1)}, bf16[256,1408]{1,0:T(8,128)(2,1)}, u32[]{:S(2)}, u32[]{:S(2)}) collective-permute-start(bf16[256,1408]{1,0:T(8,128)(2,1)} %fusion.17), channel_id=1, source_target_pairs={{0,8},{8,16},{16,24},{24,28},{28,20},{20,12},{12,4},{4,0},{1,9},{9... | collective-permute-start | bytes 2162696 | tf_op jit(solution)/shard_map/ppermute | solution.py:52
  522.8 27.0 %collective-permute-start.125 = (bf16[256,1408]{1,0:T(8,128)(2,1)}, bf16[256,1408]{1,0:T(8,128)(2,1)}, u32[]{:S(2)}, u32[]{:S(2)}) collective-permute-start(bf16[256,1408]{1,0:T(8,128)(2,1)} %fusion.20), channel_id=1, source_target_pairs={{0,4},{8,0},{16,8},{24,16},{28,24},{20,28},{12,20},{4,12},{1,5},{9... | collective-permute-start | bytes 2162696 | tf_op jit(solution)/shard_map/ppermute | solution.py:52
  527.6 26.1 %collective-permute-start.70 = (bf16[256,2048]{1,0:T(8,128)(2,1)S(1)}, bf16[256,2048]{1,0:T(8,128)(2,1)S(1)}, u32[]{:S(2)}, u32[]{:S(2)}) collective-permute-start(bf16[256,2048]{1,0:T(8,128)(2,1)S(1)} %get-tuple-element.420), channel_id=1, source_target_pairs={{0,2},{1,3},{2,0},{3,1},{4,6},{5,7},{6,4},{7,5},{8,10},{9,11},{10,... | collective-permute-start | bytes 3145736 | tf_op jit(solution)/shard_map/ppermute | solution.py:115
  530.9 47.3 %collective-permute-start.66 = (bf16[256,2048]{1,0:T(8,128)(2,1)S(1)}, bf16[256,2048]{1,0:T(8,128)(2,1)S(1)}, u32[]{:S(2)}, u32[]{:S(2)}) collective-permute-start(bf16[256,2048]{1,0:T(8,128)(2,1)S(1)} %get-tuple-element.442), channel_id=1, source_target_pairs={{0,2},{1,3},{2,0},{3,1},{4,6},{5,7},{6,4},{7,5},{8,10},{9,11},{10,... | collective-permute-start | bytes 3145736 | tf_op jit(solution)/shard_map/ppermute | solution.py:115
  534.8 46.3 %collective-permute-start.86 = (bf16[256,1408]{1,0:T(8,128)(2,1)S(1)}, bf16[256,1408]{1,0:T(8,128)(2,1)S(1)}, u32[]{:S(2)}, u32[]{:S(2)}) collective-permute-start(bf16[256,1408]{1,0:T(8,128)(2,1)S(1)} %fusion.9), channel_id=1, source_target_pairs={{0,8},{8,16},{16,24},{24,28},{28,20},{20,12},{12,4},{4,0},{1,9},{9... | collective-permute-start | bytes 2162696 | tf_op jit(solution)/shard_map/ppermute | solution.py:52
  546.4 34.7 %collective-permute-start.101 = (bf16[256,1408]{1,0:T(8,128)(2,1)S(1)}, bf16[256,1408]{1,0:T(8,128)(2,1)S(1)}, u32[]{:S(2)}, u32[]{:S(2)}) collective-permute-start(bf16[256,1408]{1,0:T(8,128)(2,1)S(1)} %fusion.12), channel_id=1, source_target_pairs={{0,4},{8,0},{16,8},{24,16},{28,24},{20,28},{12,20},{4,12},{1,5},{9... | collective-permute-start | bytes 2162696 | tf_op jit(solution)/shard_map/ppermute | solution.py:52
  549.9 23.4 %collective-permute-start.113 = (bf16[256,1408]{1,0:T(8,128)(2,1)S(1)}, bf16[256,1408]{1,0:T(8,128)(2,1)S(1)}, u32[]{:S(2)}, u32[]{:S(2)}) collective-permute-start(bf16[256,1408]{1,0:T(8,128)(2,1)S(1)} %fusion.16), channel_id=1, source_target_pairs={{0,8},{8,16},{16,24},{24,28},{28,20},{20,12},{12,4},{4,0},{1,9},{9... | collective-permute-start | bytes 2162696 | tf_op jit(solution)/shard_map/ppermute | solution.py:52
  573.3 24.1 %collective-permute-start.71 = (bf16[512,2048]{1,0:T(8,128)(2,1)S(1)}, bf16[512,2048]{1,0:T(8,128)(2,1)S(1)}, u32[]{:S(2)}, u32[]{:S(2)}) collective-permute-start(bf16[512,2048]{1,0:T(8,128)(2,1)S(1)} %pad_maximum_fusion.8), channel_id=1, source_target_pairs={{0,1},{1,0},{2,3},{3,2},{4,5},{5,4},{6,7},{7,6},{8,9},{9,8},{10,11... | collective-permute-start | bytes 6291464 | tf_op jit(solution)/shard_map/ppermute | solution.py:115
  581.1 46.7 %collective-permute-start.67 = (bf16[512,2048]{1,0:T(8,128)(2,1)}, bf16[512,2048]{1,0:T(8,128)(2,1)}, u32[]{:S(2)}, u32[]{:S(2)}) collective-permute-start(bf16[512,2048]{1,0:T(8,128)(2,1)} %pad_maximum_fusion.7), channel_id=1, source_target_pairs={{0,1},{1,0},{2,3},{3,2},{4,5},{5,4},{6,7},{7,6},{8,9},{9,8},{10,11... | collective-permute-start | bytes 6291464 | tf_op jit(solution)/shard_map/ppermute | solution.py:115
  600.2 35.7 %collective-permute-start.87 = (bf16[256,256]{1,0:T(8,128)(2,1)}, bf16[256,256]{1,0:T(8,128)(2,1)}, u32[]{:S(2)}, u32[]{:S(2)}) collective-permute-start(bf16[256,256]{1,0:T(8,128)(2,1)} %get-tuple-element.327), channel_id=1, source_target_pairs={{0,8},{8,16},{16,24},{24,28},{28,20},{20,12},{12,4},{4,0},{1,9},{9... | collective-permute-start | bytes 393224 | tf_op jit(solution)/shard_map/ppermute | solution.py:52
  601.4 38.1 %collective-permute-start.102 = (bf16[256,256]{1,0:T(8,128)(2,1)}, bf16[256,256]{1,0:T(8,128)(2,1)}, u32[]{:S(2)}, u32[]{:S(2)}) collective-permute-start(bf16[256,256]{1,0:T(8,128)(2,1)} %get-tuple-element.342), channel_id=1, source_target_pairs={{0,4},{8,0},{16,8},{24,16},{28,24},{20,28},{12,20},{4,12},{1,5},{9... | collective-permute-start | bytes 393224 | tf_op jit(solution)/shard_map/ppermute | solution.py:52
  614.3 31.3 %collective-permute-start.72 = (bf16[528,256]{1,0:T(8,128)(2,1)}, bf16[528,256]{1,0:T(8,128)(2,1)}, u32[]{:S(2)}, u32[]{:S(2)}) collective-permute-start(bf16[528,256]{1,0:T(8,128)(2,1)} %pad_maximum_fusion.12), channel_id=1, source_target_pairs={{4,0},{8,4},{12,8},{16,12},{20,16},{24,20},{28,24},{5,1},{9,5},{13... | collective-permute-start | bytes 811016 | tf_op jit(solution)/shard_map/ppermute | solution.py:163
  617.8 25.8 %collective-permute-start.128 = (bf16[128,512]{1,0:T(8,128)(2,1)}, bf16[128,512]{1,0:T(8,128)(2,1)}, u32[]{:S(2)}, u32[]{:S(2)}) collective-permute-start(bf16[128,512]{1,0:T(8,128)(2,1)} %get-tuple-element.368), channel_id=1, source_target_pairs={{0,4},{8,0},{16,8},{24,16},{28,24},{20,28},{12,20},{4,12},{1,5},{9... | collective-permute-start | bytes 393224 | tf_op jit(solution)/shard_map/ppermute | solution.py:52
  664.7 23.6 %collective-permute-start.90 = (bf16[512,256]{1,0:T(8,128)(2,1)S(1)}, bf16[512,256]{1,0:T(8,128)(2,1)S(1)}, u32[]{:S(2)}, u32[]{:S(2)}) collective-permute-start(bf16[512,256]{1,0:T(8,128)(2,1)S(1)} %fusion.25), channel_id=1, source_target_pairs={{0,8},{8,16},{16,24},{24,28},{28,20},{20,12},{12,4},{4,0},{1,9},{9... | collective-permute-start | bytes 786440 | tf_op jit(solution)/shard_map/ppermute | solution.py:52
  763.1 23.8 %collective-permute-start.77 = (bf16[256,2048]{1,0:T(8,128)(2,1)S(1)}, bf16[256,2048]{1,0:T(8,128)(2,1)S(1)}, u32[]{:S(2)}, u32[]{:S(2)}) collective-permute-start(bf16[256,2048]{1,0:T(8,128)(2,1)S(1)} %dynamic-slice_convert_fusion), channel_id=1, source_target_pairs={{0,2},{1,3},{2,0},{3,1},{4,6},{5,7},{6,4},{7,5},{8,10},{9,11},{10,... | collective-permute-start | bytes 3145736 | tf_op jit(solution)/shard_map/ppermute | solution.py:115
  765.7 24.0 %collective-permute-start.94 = (bf16[128,1152]{1,0:T(8,128)(2,1)S(1)}, bf16[128,1152]{1,0:T(8,128)(2,1)S(1)}, u32[]{:S(2)}, u32[]{:S(2)}) collective-permute-start(bf16[128,1152]{1,0:T(8,128)(2,1)S(1)} %add_convert_fusion.19), channel_id=1, source_target_pairs={{0,8},{8,16},{16,24},{24,28},{28,20},{20,12},{12,4},{4,0},{1,9},{9... | collective-permute-start | bytes 884744 | tf_op jit(solution)/shard_map/ppermute | solution.py:52
  767.2 22.4 %collective-permute-start.109 = (bf16[128,1152]{1,0:T(8,128)(2,1)S(1)}, bf16[128,1152]{1,0:T(8,128)(2,1)S(1)}, u32[]{:S(2)}, u32[]{:S(2)}) collective-permute-start(bf16[128,1152]{1,0:T(8,128)(2,1)S(1)} %add_convert_fusion.16), channel_id=1, source_target_pairs={{0,4},{8,0},{16,8},{24,16},{28,24},{20,28},{12,20},{4,12},{1,5},{9... | collective-permute-start | bytes 884744 | tf_op jit(solution)/shard_map/ppermute | solution.py:52
  788.2 22.9 %collective-permute-start.78 = (bf16[256,2048]{1,0:T(8,128)(2,1)S(1)}, bf16[256,2048]{1,0:T(8,128)(2,1)S(1)}, u32[]{:S(2)}, u32[]{:S(2)}) collective-permute-start(bf16[256,2048]{1,0:T(8,128)(2,1)S(1)} %add_convert_fusion.2), channel_id=1, source_target_pairs={{0,2},{1,3},{2,0},{3,1},{4,6},{5,7},{6,4},{7,5},{8,10},{9,11},{10,... | collective-permute-start | bytes 3145736 | tf_op jit(solution)/shard_map/ppermute | solution.py:115
  (156 other events, 2044.3 us)
